TPU v7x, 32 devices: a whole 2x2x4 slice. The times are simulated.
32 devices in a mesh: rep: 8 (over z, core), seq: 4 (over y, x).
Axes of the slice: x: 2, y: 2, z: 4, core: 2. Of those that a mesh axis runs over, the one named last changes fastest.
Arguments:
- latent: bfloat16 [768, 2432], P(('seq', 'rep')), may hold values from -50 to 50
- noise: bfloat16 [8, 768, 2432], P('rep', 'seq'), may hold values from -6 to 6
- timestep: int32 [8], P('rep'), may hold values from 10 to 989
- text_kv: bfloat16 [2, 128, 1536], P(None, None, 'seq'), may hold values from -6 to 6
- qk_gain: float32 [2, 64], replicated, may hold values from 1 to 3
- prompt: float32 [1280], replicated, may hold values from -6 to 6
- w_qkv: bfloat16 [2432, 4608], P('rep'), may hold values from -0.125 to 0.125
- a_qkv: bfloat16 [2432, 64], replicated, may hold values from -0.125 to 0.125
- b_qkv: bfloat16 [64, 4608], replicated, may hold values from -0.75 to 0.75
- w_out: bfloat16 [1536, 2432], P('rep'), may hold values from -0.15625 to 0.15625
- a_out: bfloat16 [1536, 64], replicated, may hold values from -0.15625 to 0.15625
- b_out: bfloat16 [64, 2432], replicated, may hold values from -0.75 to 0.75
- w_patch: bfloat16 [2432, 1280], replicated, may hold values from -0.125 to 0.125
Outputs:
- rewards: float32 [8], P('rep')
- latent_grad: float32 [768, 2432], P(('seq', 'rep'))
- grad_a_qkv: float32 [2432, 64], P('rep')
- grad_b_qkv: float32 [64, 4608], P(None, 'rep')
- grad_a_out: float32 [1536, 64], P('rep')
- grad_b_out: float32 [64, 2432], P(None, 'rep')
All inputs are finite; a program needn't handle non-finite values.
Results may differ from a plain program's by a relative error of at most 0.024.
Values may be sent and summed in bfloat16 or wider, within the bound.
A program may use at most 192 MiB of HBM per device.

v0:
```python
import math

import jax
import jax.numpy as jnp
from jax import lax
from jax.sharding import PartitionSpec as P

HEAD_DIM = 64


epsilon = 1e-06
logit_scale = 100.0
contract_last = (((1,), (1,)), ((), ()))
contract_first = (((0,), (0,)), ((), ()))


def layer_norm(mixed_in):
    centred = mixed_in - jnp.mean(mixed_in, axis=-1, keepdims=True)
    return centred * lax.rsqrt(jnp.mean(centred * centred, axis=-1, keepdims=True) + epsilon)


def head_norm(values_in, norm_gain, head_size):
    leading = values_in.shape[0]
    shaped = values_in.reshape(leading, -1, head_size)
    scaled = shaped * lax.rsqrt(jnp.mean(shaped * shaped, axis=-1, keepdims=True) + epsilon)
    return (scaled * norm_gain).reshape(leading, -1)


def split_heads(matrix, head_size):
    return jnp.transpose(matrix.reshape(matrix.shape[0], -1, head_size), (1, 0, 2))


def merge_heads(blocks):
    return jnp.transpose(blocks, (1, 0, 2)).reshape(blocks.shape[1], -1)


def project_in(latent_rows, noise_rows, noise_level, w_qkv, a_qkv, b_qkv, qk_gain, head_size):
    mixed_in = (1.0 - noise_level) * latent_rows.astype(
        jnp.float32
    ) + noise_level * noise_rows.astype(jnp.float32)
    normed = layer_norm(mixed_in).astype(jnp.bfloat16)
    low_rank = jnp.dot(normed, a_qkv, preferred_element_type=jnp.float32).astype(jnp.bfloat16)
    joined_qkv = jnp.dot(normed, w_qkv, preferred_element_type=jnp.float32) + jnp.dot(
        low_rank, b_qkv, preferred_element_type=jnp.float32
    )
    inner_width = joined_qkv.shape[1] // 3
    query_part = head_norm(joined_qkv[:, :inner_width], qk_gain[0], head_size)
    key_part = head_norm(joined_qkv[:, inner_width : 2 * inner_width], qk_gain[1], head_size)
    stacked = jnp.stack([query_part, key_part, joined_qkv[:, 2 * inner_width :]], axis=1).astype(
        jnp.bfloat16
    )
    return (mixed_in, normed, low_rank, joined_qkv, stacked)


def head_scores(query_head, key_head, head_size):
    logits = lax.dot_general(
        query_head, key_head, contract_last, preferred_element_type=jnp.float32
    ) / math.sqrt(head_size)
    expped = jnp.exp(logits)
    return expped / jnp.sum(expped, axis=1, keepdims=True)


def attend(stacked, text_keys, text_values, head_size):
    query_heads = split_heads(stacked[:, 0], head_size)
    key_heads = split_heads(jnp.concatenate([stacked[:, 1], text_keys], axis=0), head_size)
    value_heads = split_heads(jnp.concatenate([stacked[:, 2], text_values], axis=0), head_size)

    def one_head(inputs):
        query_head, key_head, value_head = inputs
        rounded = head_scores(query_head, key_head, head_size).astype(jnp.bfloat16)
        return jnp.dot(rounded, value_head, preferred_element_type=jnp.float32).astype(jnp.bfloat16)

    return merge_heads(lax.map(one_head, (query_heads, key_heads, value_heads)))


def attend_back(stacked, text_keys, text_values, grad_attended, head_size):
    tokens_all = stacked.shape[0]
    query_heads = split_heads(stacked[:, 0], head_size)
    key_heads = split_heads(jnp.concatenate([stacked[:, 1], text_keys], axis=0), head_size)
    value_heads = split_heads(jnp.concatenate([stacked[:, 2], text_values], axis=0), head_size)
    grad_heads = split_heads(grad_attended, head_size)

    def one_head(inputs):
        query_head, key_head, value_head, grad_head = inputs
        soft_probs = head_scores(query_head, key_head, head_size)
        rounded = soft_probs.astype(jnp.bfloat16)
        grad_values = lax.dot_general(
            rounded, grad_head, contract_first, preferred_element_type=jnp.float32
        )
        grad_probs = lax.dot_general(
            grad_head, value_head, contract_last, preferred_element_type=jnp.float32
        )
        centre = jnp.sum(soft_probs * grad_probs, axis=1, keepdims=True)
        grad_logits = (soft_probs * (grad_probs - centre) / math.sqrt(head_size)).astype(
            jnp.bfloat16
        )
        grad_query = jnp.dot(grad_logits, key_head, preferred_element_type=jnp.float32)
        grad_keys = lax.dot_general(
            grad_logits, query_head, contract_first, preferred_element_type=jnp.float32
        )
        return jnp.stack([grad_query, grad_keys[:tokens_all], grad_values[:tokens_all]], axis=0)

    per_head = lax.map(one_head, (query_heads, key_heads, value_heads, grad_heads))
    return jnp.transpose(per_head, (2, 1, 0, 3)).reshape(tokens_all, 3, -1).astype(jnp.bfloat16)


def project_out(attended, mixed_in, noise_level, w_out, a_out, b_out, w_patch):
    low_out = jnp.dot(attended, a_out, preferred_element_type=jnp.float32).astype(jnp.bfloat16)
    velocity = jnp.dot(attended, w_out, preferred_element_type=jnp.float32) + jnp.dot(
        low_out, b_out, preferred_element_type=jnp.float32
    )
    denoised = (mixed_in - noise_level * velocity).astype(jnp.bfloat16)
    patch_pre = jnp.dot(denoised, w_patch, preferred_element_type=jnp.float32)
    return (low_out, patch_pre, jnp.sum(jax.nn.gelu(patch_pre), axis=0))


def reward(pooled, prompt):
    return (
        logit_scale
        * jnp.sum(pooled * prompt)
        * lax.rsqrt(jnp.sum(pooled * pooled) + epsilon)
        * lax.rsqrt(jnp.sum(prompt * prompt) + epsilon)
    )


def backward_out(
    patch_pre, grad_pooled, noise_level, attended, low_out, w_out, a_out, b_out, w_patch
):
    gelu_back = jax.vjp(jax.nn.gelu, patch_pre)[1]
    grad_pre = gelu_back(jnp.broadcast_to(grad_pooled, patch_pre.shape))[0].astype(jnp.bfloat16)
    grad_denoised = lax.dot_general(
        grad_pre, w_patch, contract_last, preferred_element_type=jnp.float32
    )
    grad_velocity = (-noise_level * grad_denoised).astype(jnp.bfloat16)
    grad_low_out = lax.dot_general(
        grad_velocity, b_out, contract_last, preferred_element_type=jnp.float32
    ).astype(jnp.bfloat16)
    grad_attended = (
        lax.dot_general(grad_velocity, w_out, contract_last, preferred_element_type=jnp.float32)
        + lax.dot_general(grad_low_out, a_out, contract_last, preferred_element_type=jnp.float32)
    ).astype(jnp.bfloat16)
    grad_a_out = lax.dot_general(
        attended, grad_low_out, contract_first, preferred_element_type=jnp.float32
    )
    grad_b_out = lax.dot_general(
        low_out, grad_velocity, contract_first, preferred_element_type=jnp.float32
    )
    return (grad_denoised, grad_attended, grad_a_out, grad_b_out)


def backward_in(
    mixed_in,
    normed,
    low_rank,
    joined_qkv,
    grad_stacked,
    noise_level,
    w_qkv,
    a_qkv,
    b_qkv,
    qk_gain,
    head_size,
    grad_denoised,
):
    inner_width = joined_qkv.shape[1] // 3
    query_back = jax.vjp(
        lambda section: head_norm(section, qk_gain[0], head_size), joined_qkv[:, :inner_width]
    )[1]
    key_back = jax.vjp(
        lambda section: head_norm(section, qk_gain[1], head_size),
        joined_qkv[:, inner_width : 2 * inner_width],
    )[1]
    grad_joined = jnp.concatenate(
        [
            query_back(grad_stacked[:, 0].astype(jnp.float32))[0],
            key_back(grad_stacked[:, 1].astype(jnp.float32))[0],
            grad_stacked[:, 2].astype(jnp.float32),
        ],
        axis=1,
    ).astype(jnp.bfloat16)
    grad_low = lax.dot_general(
        grad_joined, b_qkv, contract_last, preferred_element_type=jnp.float32
    ).astype(jnp.bfloat16)
    grad_normed = lax.dot_general(
        grad_joined, w_qkv, contract_last, preferred_element_type=jnp.float32
    ) + lax.dot_general(grad_low, a_qkv, contract_last, preferred_element_type=jnp.float32)
    grad_mixed = jax.vjp(layer_norm, mixed_in)[1](grad_normed)[0] + grad_denoised
    grad_latent = (1.0 - noise_level) * grad_mixed
    grad_a_qkv = lax.dot_general(
        normed, grad_low, contract_first, preferred_element_type=jnp.float32
    )
    grad_b_qkv = lax.dot_general(
        low_rank, grad_joined, contract_first, preferred_element_type=jnp.float32
    )
    return (grad_latent, grad_a_qkv, grad_b_qkv)


def shards(
    latent,
    noise,
    timestep,
    text_kv,
    qk_gain,
    prompt,
    w_qkv,
    a_qkv,
    b_qkv,
    w_out,
    a_out,
    b_out,
    w_patch,
):
    latent_rows, weight_in, weight_back = (
        lax.all_gather(latent, "rep", axis=0, tiled=True),
        lax.all_gather(w_qkv, "rep", axis=0, tiled=True),
        lax.all_gather(w_out, "rep", axis=0, tiled=True),
    )
    noise_level = timestep[0].astype(jnp.float32) / 1000.0
    text_keys = head_norm(text_kv[0].astype(jnp.float32), qk_gain[1], HEAD_DIM).astype(jnp.bfloat16)
    text_values = text_kv[1]
    mixed_in, normed, low_rank, joined_qkv, stacked = project_in(
        latent_rows, noise[0], noise_level, weight_in, a_qkv, b_qkv, qk_gain, HEAD_DIM
    )
    by_head = lax.all_to_all(stacked, "seq", split_axis=2, concat_axis=0, tiled=True)
    attended_heads = attend(by_head, text_keys, text_values, HEAD_DIM)
    attended = lax.all_to_all(attended_heads, "seq", split_axis=0, concat_axis=1, tiled=True)
    low_out, patch_pre, partial_sum = project_out(
        attended, mixed_in, noise_level, weight_back, a_out, b_out, w_patch
    )
    summed = lax.psum(partial_sum, "seq")
    pooled = summed / (latent_rows.shape[0] * lax.axis_size("seq"))
    score_value, grad_pooled = jax.value_and_grad(reward)(pooled, prompt)
    grad_denoised, grad_attended, grad_a_out, grad_b_out = backward_out(
        patch_pre, grad_pooled, noise_level, attended, low_out, weight_back, a_out, b_out, w_patch
    )
    grad_heads = lax.all_to_all(grad_attended, "seq", split_axis=1, concat_axis=0, tiled=True)
    grad_by_head = attend_back(by_head, text_keys, text_values, grad_heads, HEAD_DIM)
    grad_stacked = lax.all_to_all(grad_by_head, "seq", split_axis=0, concat_axis=2, tiled=True)
    grad_latent, grad_a_qkv, grad_b_qkv = backward_in(
        mixed_in,
        normed,
        low_rank,
        joined_qkv,
        grad_stacked,
        noise_level,
        weight_in,
        a_qkv,
        b_qkv,
        qk_gain,
        HEAD_DIM,
        grad_denoised,
    )
    latent_grad = lax.psum_scatter(
        grad_latent.astype(jnp.bfloat16), "rep", scatter_dimension=0, tiled=True
    ).astype(jnp.float32)
    shard_a_qkv, shard_b_qkv, shard_a_out, shard_b_out = (
        lax.psum_scatter(
            grad_a_qkv.astype(jnp.bfloat16), "rep", scatter_dimension=0, tiled=True
        ).astype(jnp.float32),
        lax.psum_scatter(
            grad_b_qkv.astype(jnp.bfloat16), "rep", scatter_dimension=1, tiled=True
        ).astype(jnp.float32),
        lax.psum_scatter(
            grad_a_out.astype(jnp.bfloat16), "rep", scatter_dimension=0, tiled=True
        ).astype(jnp.float32),
        lax.psum_scatter(
            grad_b_out.astype(jnp.bfloat16), "rep", scatter_dimension=1, tiled=True
        ).astype(jnp.float32),
    )
    shard_a_qkv, shard_b_qkv, shard_a_out, shard_b_out = (
        lax.psum(shard_a_qkv.astype(jnp.bfloat16), "seq").astype(jnp.float32),
        lax.psum(shard_b_qkv.astype(jnp.bfloat16), "seq").astype(jnp.float32),
        lax.psum(shard_a_out.astype(jnp.bfloat16), "seq").astype(jnp.float32),
        lax.psum(shard_b_out.astype(jnp.bfloat16), "seq").astype(jnp.float32),
    )
    return (score_value.reshape(1), latent_grad, shard_a_qkv, shard_b_qkv, shard_a_out, shard_b_out)


def solution(mesh):
    in_specs = (
        P(("seq", "rep"), None),
        P("rep", "seq", None),
        P("rep"),
        P(None, None, "seq"),
        P(),
        P(),
        P("rep", None),
        P(),
        P(),
        P("rep", None),
        P(),
        P(),
        P(),
    )
    out_specs = (
        P("rep"),
        P(("seq", "rep"), None),
        P("rep", None),
        P(None, "rep"),
        P("rep", None),
        P(None, "rep"),
    )
    return jax.shard_map(shards, mesh=mesh, in_specs=in_specs, out_specs=out_specs, check_vma=False)
```

profile of v0, /device:TPU:0, one launch (start us, length us, event | category | flops | bytes accessed | tf_op | source)
XLA Modules:
  0.0 746.1 jit_solution(5077723040433768150)
XLA Ops:
  10.0 17.9 %all_gather.9 = bf16[192,2432]{1,0:T(8,128)(2,1)S(1)} all-gather(bf16[24,2432]{1,0:T(8,128)(2,1)S(1)} %copy-done.18), channel_id=1, replica_groups=mesh['rep'=8,'seq'=4] {'rep'}, dimensions={0}, use_global_device_ids=true | all-gather | bytes 1050624 | tf_op jit(solution)/shard_map/all_gather | solution.py:214
  31.0 178.8 %all-gather.3.cloned.1.call-done = bf16[2432,4608]{1,0:T(8,128)(2,1)} async-done(((bf16[304,4608]{1,0:T(8,128)(2,1)}), bf16[2432,4608]{1,0:T(8,128)(2,1)}) %all-gather.3.cloned.1.call-update) | async-done | bytes 22413328 | tf_op jit(solution)/shard_map/all_gather | solution.py:215
  209.8 10.0 %fusion.97 = f32[192,4608]{1,0:T(8,128)S(1)} fusion(bf16[192,2432]{1,0:T(8,128)(2,1)S(1)} %multiply_convert_fusion.3, bf16[2432,4608]{1,0:T(8,128)(2,1)} %all-gather.3.cloned.1.call-done), kind=kOutput, calls=%fused_computation.160 | convolution fusion | flops 4303355904 | bytes 26886144 | tf_op jit(solution)/shard_map/dot_general | solution.py:43
  223.0 2.9 copy.78
  228.8 3.0 copy.79
  231.7 2.9 copy.80
  237.6 2.9 copy.81
  242.1 2.5 fusion.65
  246.0 5.5 copy.82
  251.4 4.8 all-to-all-start
  261.1 31.9 %all-to-all-done = bf16[192,3,1536]{0,1,2:T(4,128)(2,1)} async-done(((bf16[192,3,1536]{0,1,2:T(4,128)(2,1)}), bf16[192,3,1536]{0,1,2:T(4,128)(2,1)}, u32[]{:S(2)}, u32[]{:S(2)}) %all-to-all-start) | async-done | bytes 1769504 | tf_op jit(solution)/shard_map/all_to_all | solution.py:224
  293.0 5.5 copy.84
  298.5 2.8 fusion.95
  301.3 2.1 copy.88
  303.4 2.1 copy.86
  305.6 2.1 copy.85
  307.7 2.3 copy.90
  310.0 2.1 maximum_bitcast_fusion.1
  312.1 2.4 copy.91
  316.5 2.4 copy.92
  318.9 23.6 %while.20 = (s32[]{:T(128)}, bf16[6,768,64]{1,2,0:T(8,128)(2,1)}, bf16[6,768,64]{2,1,0:T(8,128)(2,1)}, bf16[6,896,64]{2,1,0:T(8,128)(2,1)}, bf16[6,896,64]{2,1,0:T(8,128)(2,1)}, /*index=5*/s32[]{:T(128)}) while((s32[]{:T(128)}, bf16[6,768,64]{1,2,0:T(8,128)(2,1)}, bf16[6,768,64]{2,1,0:T(8,128)(2,1)}, bf16[6,896,64]{2,1,0:T(8,128)(2,1)}, ...), condition=%wide.region_7.8_spmd, body=%wide.region_5.7_spmd.sunk | while | flops 179649792 | bytes 6266957 | solution.py:73
  320.6 2.3 fusion.146
  324.5 2.3 fusion.146
  328.4 2.2 fusion.146
  332.4 2.3 fusion.146
  336.3 2.2 fusion.146
  340.2 2.2 fusion.146
  342.5 2.9 all_to_all.56
  345.4 2.1 copy.93
  347.5 4.2 all-to-all-start.1
  351.7 8.7 %all-to-all-done.1 = bf16[4,192,384]{2,1,0:T(8,128)(2,1)} async-done(((bf16[4,192,384]{2,1,0:T(8,128)(2,1)}), bf16[4,192,384]{2,1,0:T(8,128)(2,1)}, u32[]{:S(2)}, u32[]{:S(2)}) %all-to-all-start.1) | async-done | bytes 589856 | tf_op jit(solution)/shard_map/all_to_all | solution.py:226
  363.6 6.3 fusion.98
  369.9 6.2 fusion.63
  376.1 9.1 %psum.35 = f32[1280]{0:T(1024)S(1)} all-reduce(f32[1280]{0:T(1024)S(1)} %get-tuple-element.155), channel_id=1, replica_groups=mesh['rep'=8,'seq'=4] {'seq'}, use_global_device_ids=true, to_apply=%region_9.10 | all-reduce | flops 1280 | bytes 10240 | tf_op jit(solution)/shard_map/psum | solution.py:230
  387.9 6.7 multiply_convert_fusion.2
  395.1 5.7 fusion.99
  402.0 4.4 all-to-all-start.2
  406.4 6.8 all-to-all-done.2
  413.2 2.2 copy.96
  415.4 2.7 reshape.182
  418.1 53.2 %while.21 = (s32[]{:T(128)}, bf16[6,3,768,64]{2,3,0,1:T(8,128)(2,1)}, bf16[6,768,64]{2,1,0:T(8,128)(2,1)}, bf16[6,896,64]{2,1,0:T(8,128)(2,1)}, bf16[6,768,64]{1...) while((s32[]{:T(128)}, bf16[6,3,768,64]{2,3,0,1:T(8,128)(2,1)}, ...), condition=%wide.region_16.17_spmd, body=%wide.region_13.16_spmd.sunk | while | flops 423000576 | bytes 23804004 | solution.py:103
  471.3 5.2 copy.102
  476.4 4.6 all-to-all-start.3
  485.0 2.2 convolution_convert_fusion.2
  487.2 2.0 copy.119
  489.3 15.6 %all-to-all-done.3 = bf16[768,3,384]{2,1,0:T(4,128)(2,1)} async-done(((bf16[768,3,384]{2,1,0:T(4,128)(2,1)}), bf16[768,3,384]{2,1,0:T(4,128)(2,1)}, u32[]{:S(2)}, u32[]{:S(2)}) %all-to-all-start.3) | async-done | bytes 1769504 | tf_op jit(solution)/shard_map/all_to_all | solution.py:238
  509.2 2.9 copy.106
  512.1 2.9 copy.109
  515.0 3.7 multiply_reduce_fusion.3
  520.2 2.9 copy.107
  524.4 2.9 copy.110
  527.3 4.4 fusion.50
  533.8 2.1 copy.113
  537.5 9.2 %reduce-scatter.22.cloned.1.call-done = bf16[304,64]{1,0:T(8,128)(2,1)} async-done(((bf16[2432,64]{1,0:T(8,128)(2,1)}), bf16[304,64]{1,0:T(8,128)(2,1)}) %reduce-scatter.22.cloned.1.call-update) | async-done | bytes 38928
  548.2 2.7 convolution_convert_fusion
  550.9 2.4 copy.115
  553.7 13.5 %fusion.91 = f32[192,2432]{1,0:T(8,128)} fusion(bf16[2432,4608]{1,0:T(8,128)(2,1)} %all-gather.3.cloned.1.call-done, bf16[192,1536]{1,0:T(8,128)(2,1)S(1)} %copy-done.11, bf16[192,1536]{1,0:T(8,128)(2,1)} %copy-done.13, bf16[192,1536]{1,0:T(8,128)(2,1)} %copy-done.12), kind=kOutput, calls=%fused_computation.155 | convolution fusion | flops 4308664320 | bytes 26050560 | tf_op jit(solution)/shard_map/dot_general | solution.py:184
  567.2 2.3 multiply_reduce_fusion.1
  571.5 6.8 reduce-scatter.16.cloned.1.call-done
  580.0 31.7 %reduce-scatter.18.cloned.1.call-done = bf16[576,64]{1,0:T(8,128)(2,1)} async-done(((bf16[4608,64]{1,0:T(8,128)(2,1)}), bf16[576,64]{1,0:T(8,128)(2,1)}) %reduce-scatter.18.cloned.1.call-update) | async-done | bytes 73744
  613.4 3.3 multiply_convert_fusion.1
  616.7 39.7 %all-reduce.7.cloned.1.call-done = (bf16[304,64]{0,1:T(8,128)(2,1)}, bf16[192,64]{0,1:T(8,128)(2,1)}, bf16[64,304]{1,0:T(8,128)(2,1)}) async-done(((bf16[304,64]{0,1:T(8,128)(2,1)}, bf16[192,64]{0,1:T(8,128)(2,1)}, bf16[64,304]{1,0:T(8,128)(2,1)}), (bf16[304,64]{0,1:T(8,128)(2,1)}, bf16[192,64]{0,1:T(8,128)(2,1)}, bf16[64,304]{1,0:T(8,128)(2,1)})) %all-reduce.7.cloned.1.call-update) | async-done | bytes 102416 | tf_op jit(solution)/shard_map/psum | solution.py:271
  660.8 40.3 %all-reduce.5.cloned.1.call-done = bf16[64,576]{1,0:T(8,128)(2,1)} async-done(((bf16[64,576]{1,0:T(8,128)(2,1)}), bf16[64,576]{1,0:T(8,128)(2,1)}) %all-reduce.5.cloned.1.call-update) | async-done | bytes 73744 | tf_op jit(solution)/shard_map/psum | solution.py:272
  702.6 34.2 %reduce-scatter.24.cloned.1.call-done = bf16[24,2432]{1,0:T(8,128)(2,1)} async-done(((bf16[192,2432]{1,0:T(8,128)(2,1)}), bf16[24,2432]{1,0:T(8,128)(2,1)}) %reduce-scatter.24.cloned.1.call-update) | async-done | bytes 116752
  (190 shorter events, 121.8 us)
Async XLA Ops:
  7.2 212.7 %copy-start = (bf16[64,4608]{1,0:T(8,128)(2,1)S(1)}, bf16[64,4608]{1,0:T(8,128)(2,1)}, u32[]{:S(2)}) copy-start(bf16[64,4608]{1,0:T(8,128)(2,1)} %param.25) | copy-start | bytes 1769476
  7.2 2.2 copy-start.30
  7.2 2.8 copy-start.18
  7.2 20.7 %copy-start.2 = (bf16[1,192,2432]{2,1,0:T(8,128)(2,1)S(1)}, bf16[1,192,2432]{2,1,0:T(8,128)(2,1)}, u32[]{:S(2)}) copy-start(bf16[1,192,2432]{2,1,0:T(8,128)(2,1)} %param.18) | copy-start | bytes 2801668
  7.2 202.6 %all-gather.3.cloned.1.call-start = ((), (), s32[]{:S(2)}) async-start(), calls=%async_computation.9 | async-start | bytes 25214976 | tf_op jit(solution)/shard_map/all_gather | solution.py:215
  7.9 355.7 %all-gather.5.cloned.1.call-start = ((), (), s32[]{:S(2)}) async-start(), calls=%async_computation.10 | async-start | bytes 8404992 | tf_op jit(solution)/shard_map/all_gather | solution.py:216
  9.4 0.5 copy-start.26
  9.4 0.5 copy-start.28
  28.4 0.6 copy-start.20
  28.9 0.6 copy-start.22
  28.9 1.7 copy-start.7
  29.5 0.6 copy-start.24
  31.0 188.8 %copy-start.16 = (bf16[192,64]{0,1:T(8,128)(2,1)}, bf16[192,64]{0,1:T(8,128)(2,1)S(1)}, u32[]{:S(2)}) copy-start(bf16[192,64]{0,1:T(8,128)(2,1)S(1)} %convolution_convert_fusion.6) | copy-start | bytes 73732
  220.5 2.5 copy-start.1
  240.4 1.6 copy-start.4
  251.4 41.6 %all-to-all-start = ((bf16[192,3,1536]{0,1,2:T(4,128)(2,1)}), bf16[192,3,1536]{0,1,2:T(4,128)(2,1)}, u32[]{:S(2)}, u32[]{:S(2)}) async-start(bf16[192,3,1536]{0,1,2:T(4,128)(2,1)} %copy.82), calls=%async_computation | async-start | bytes 6291456 | tf_op jit(solution)/shard_map/all_to_all | solution.py:224
  310.0 4.5 copy-start.14
  347.5 12.9 %all-to-all-start.1 = ((bf16[4,192,384]{2,1,0:T(8,128)(2,1)}), bf16[4,192,384]{2,1,0:T(8,128)(2,1)}, u32[]{:S(2)}, u32[]{:S(2)}) async-start(bf16[4,192,384]{2,1,0:T(8,128)(2,1)} %copy.93), calls=%async_computation.1 | async-start | bytes 1179648 | tf_op jit(solution)/shard_map/all_to_all | solution.py:226
  361.5 0.8 copy-start.5
  369.9 15.3 %copy-start.19 = (f32[1280]{0:T(1024)S(1)}, f32[1280]{0:T(1024)}, u32[]{:S(2)}) copy-start(f32[1280]{0:T(1024)} %param.22) | copy-start | bytes 15364
  387.9 6.7 copy-start.15
  394.6 6.2 copy-start.6
  395.0 5.8 copy-start.9
  402.0 11.2 %all-to-all-start.2 = ((bf16[192,4,384]{2,0,1:T(8,128)(2,1)}), bf16[192,4,384]{2,0,1:T(8,128)(2,1)}, u32[]{:S(2)}, u32[]{:S(2)}) async-start(bf16[192,4,384]{2,0,1:T(8,128)(2,1)} %bitcast.239), calls=%async_computation.2 | async-start | bytes 1179648 | tf_op jit(solution)/shard_map/all_to_all | solution.py:236
  476.4 28.4 %all-to-all-start.3 = ((bf16[768,3,384]{2,1,0:T(4,128)(2,1)}), bf16[768,3,384]{2,1,0:T(4,128)(2,1)}, u32[]{:S(2)}, u32[]{:S(2)}) async-start(bf16[768,3,384]{2,1,0:T(4,128)(2,1)} %copy.102), calls=%async_computation.3 | async-start | bytes 4718592 | tf_op jit(solution)/shard_map/all_to_all | solution.py:238
  481.0 54.9 %reduce-scatter.20.cloned.1.call-start = ((), (), s32[]{:S(2)}) async-start(), calls=%async_computation.14 | async-start | bytes 442368
  484.9 61.7 %reduce-scatter.22.cloned.1.call-start = ((), (), s32[]{:S(2)}) async-start(), calls=%async_computation.15 | async-start | bytes 700416
  489.2 89.1 %reduce-scatter.16.cloned.1.call-start = ((), (), s32[]{:S(2)}) async-start(), calls=%async_computation.12 | async-start | bytes 700416
  507.0 2.2 copy-start.3
  512.1 2.9 copy-start.27
  512.1 2.9 copy-start.29
  527.3 4.4 copy-start.10
  531.7 0.8 copy-start.12
  531.7 1.0 copy-start.13
  532.7 15.5 %copy-start.17 = (bf16[192,64]{0,1:T(8,128)(2,1)S(1)}, bf16[192,64]{0,1:T(8,128)(2,1)}, u32[]{:S(2)}) copy-start(bf16[192,64]{0,1:T(8,128)(2,1)} %copy-done.16) | copy-start | bytes 73732
  535.9 75.8 %reduce-scatter.18.cloned.1.call-start = ((), (), s32[]{:S(2)}) async-start(), calls=%async_computation.13 | async-start | bytes 1327104
  550.9 2.8 copy-start.11
  553.3 13.9 %copy-start.8 = (bf16[2432,64]{0,1:T(8,128)(2,1)S(1)}, bf16[2432,64]{0,1:T(8,128)(2,1)}, u32[]{:S(2)}) copy-start(bf16[2432,64]{0,1:T(8,128)(2,1)} %param.24) | copy-start | bytes 933892
  553.3 13.8 %copy-start.21 = (f32[192]{0:T(256)S(1)}, f32[192]{0:T(256)}, u32[]{:S(2)}) copy-start(f32[192]{0:T(256)} %copy-done.20) | copy-start | bytes 2308
  553.3 103.1 %all-reduce.7.cloned.1.call-start = ((), (), s32[]{:S(2)}) async-start(), calls=%async_computation.17 | async-start | bytes 262144 | tf_op jit(solution)/shard_map/psum | solution.py:271
  567.2 2.3 copy-start.23
  567.2 2.3 copy-start.25
  579.9 121.1 %all-reduce.5.cloned.1.call-start = ((), (), s32[]{:S(2)}) async-start(), calls=%async_computation.11 | async-start | bytes 163840 | tf_op jit(solution)/shard_map/psum | solution.py:272
  613.4 123.4 %reduce-scatter.24.cloned.1.call-start = ((), (), s32[]{:S(2)}) async-start(), calls=%async_computation.16 | async-start | bytes 1050624
Sparse Core Ops, SparseCore 0:
  9.7 200.0 all-gather.2
  211.5 73.2 all-gather.4
  485.1 29.8 reduce-scatter.19
  517.2 29.3 reduce-scatter.21
  548.8 29.4 reduce-scatter.15
  580.5 31.0 reduce-scatter.17
  615.7 40.7 all-reduce.6
  660.0 41.0 all-reduce.4
  703.5 33.2 reduce-scatter.23
where the time goes:
time: 749 us; the launch traced here: 746 us
  waiting for transfers between devices  405 us (54%)
  matrix products  132 us (18%)
  local copies, waits for them, and re-layouts  100 us (13%)
  other arithmetic  44.5 us (6%)
  blocking collectives  27 us (4%)
  starting transfers between devices  18.5 us (2%)
  between operations  18.3 us (2%)
    all_gather x1, waiting for transfers between devices, shards(): lax.all_gather(w_qkv, 'rep', axis=0, tiled=True)  179 us
    unnamed x14, waiting for transfers between devices  83.3 us
    psum x1, waiting for transfers between devices, shards(): lax.psum(shard_b_qkv.astype(jnp.bfloat16), 'seq').astype(jnp.float32)  40.3 us
    psum x1, waiting for transfers between devices, shards(): lax.psum(shard_a_qkv.astype(jnp.bfloat16), 'seq').astype(jnp.float32)  39.7 us
    all_to_all x1, waiting for transfers between devices, shards(): lax.all_to_all(stacked, 'seq', split_axis=2, concat_axis=0, tiled=True)  31.9 us
    unnamed x72, local copies, waits for them, and re-layouts  20.6 us
    dot_general x12, matrix products, head_scores(): lax.dot_general(query_head, key_head, contract_last, preferred_element_ty...  20.2 us
    all_gather x1, blocking collectives, shards(): lax.all_gather(latent, 'rep', axis=0, tiled=True)  17.9 us
  transfers between devices with their start and end apart: 13, of which 11 were waited for; matrix products, arithmetic and copies ran while one was open for 24% of the time, Pallas kernels for 0%

commit v1 on v0

v1 whole, which is shorter than its diff:
```python
import functools

import jax
import jax.numpy as jnp
from jax import lax
from jax.experimental import pallas as pl
from jax.experimental.pallas import tpu as pltpu
from jax.sharding import PartitionSpec as P

HEAD_DIM = 64


epsilon = 1e-06
logit_scale = 100.0
contract_last = (((1,), (1,)), ((), ()))
contract_first = (((0,), (0,)), ((), ()))


def project_out(attended, mixed_in, noise_level, w_out, a_out, b_out, w_patch):
    low_out = jnp.dot(attended, a_out, preferred_element_type=jnp.float32).astype(jnp.bfloat16)
    velocity = jnp.dot(attended, w_out, preferred_element_type=jnp.float32) + jnp.dot(
        low_out, b_out, preferred_element_type=jnp.float32
    )
    denoised = (mixed_in - noise_level * velocity).astype(jnp.bfloat16)
    patch_pre = jnp.dot(denoised, w_patch, preferred_element_type=jnp.float32)
    return (low_out, patch_pre, jnp.sum(jax.nn.gelu(patch_pre), axis=0))


def reward(pooled, prompt):
    return (
        logit_scale
        * jnp.sum(pooled * prompt)
        * lax.rsqrt(jnp.sum(pooled * pooled) + epsilon)
        * lax.rsqrt(jnp.sum(prompt * prompt) + epsilon)
    )


def backward_out(
    patch_pre, grad_pooled, noise_level, attended, low_out, w_out, a_out, b_out, w_patch
):
    gelu_back = jax.vjp(jax.nn.gelu, patch_pre)[1]
    grad_pre = gelu_back(jnp.broadcast_to(grad_pooled, patch_pre.shape))[0].astype(jnp.bfloat16)
    grad_denoised = lax.dot_general(
        grad_pre, w_patch, contract_last, preferred_element_type=jnp.float32
    )
    grad_velocity = (-noise_level * grad_denoised).astype(jnp.bfloat16)
    grad_low_out = lax.dot_general(
        grad_velocity, b_out, contract_last, preferred_element_type=jnp.float32
    ).astype(jnp.bfloat16)
    grad_attended = (
        lax.dot_general(grad_velocity, w_out, contract_last, preferred_element_type=jnp.float32)
        + lax.dot_general(grad_low_out, a_out, contract_last, preferred_element_type=jnp.float32)
    ).astype(jnp.bfloat16)
    grad_a_out = lax.dot_general(
        attended, grad_low_out, contract_first, preferred_element_type=jnp.float32
    )
    grad_b_out = lax.dot_general(
        grad_velocity, low_out, contract_first, preferred_element_type=jnp.float32
    )
    return (grad_denoised, grad_attended, grad_a_out, grad_b_out)


MESH = pl.DeviceIdType.MESH
VMEM_LIMIT = 56 * 1024 * 1024
SCALE = HEAD_DIM**-0.5


def normalize(x, gain):
    return x * lax.rsqrt(jnp.mean(x * x, axis=-1, keepdims=True) + epsilon) * gain


def per_head(width):
    return [slice(at, at + HEAD_DIM) for at in range(0, width, HEAD_DIM)]


def attend_kernel(joined_ref, text_ref, gain_ref, att_ref, q_ref, k_ref, v_ref, inv_ref, vt, att_t):
    tokens, width = att_ref.shape
    text = text_ref.shape[1]
    chunk = inv_ref.shape[2]
    gain_q, gain_k = gain_ref[0:1], gain_ref[1:2]
    k_ref[pl.ds(tokens, text), :] = jnp.concatenate(
        [normalize(text_ref[0, :, h].astype(jnp.float32), gain_k) for h in per_head(width)], axis=1
    ).astype(jnp.bfloat16)
    v_ref[pl.ds(tokens, text), :] = text_ref[1]

    @pl.loop(0, tokens // chunk)
    def _(step):
        rows = pl.ds(pl.multiple_of(step * chunk, chunk), chunk)
        part = joined_ref[rows, :]
        q_ref[rows, :] = (
            jnp.concatenate(
                [normalize(part[:, h], gain_q) for h in per_head(width)], axis=1
            ).astype(jnp.bfloat16)
            * SCALE
        ).astype(jnp.bfloat16)
        k_ref[rows, :] = jnp.concatenate(
            [normalize(part[:, width : 2 * width][:, h], gain_k) for h in per_head(width)], axis=1
        ).astype(jnp.bfloat16)
        v_ref[rows, :] = part[:, 2 * width :].astype(jnp.bfloat16)

    vt[...] = v_ref[...].astype(jnp.float32).T.astype(jnp.bfloat16)

    @pl.loop(0, tokens // chunk)
    def _(step):
        rows = pl.ds(pl.multiple_of(step * chunk, chunk), chunk)
        for number, h in enumerate(per_head(width)):
            scores = lax.dot_general(
                k_ref[:, h], q_ref[rows, h], contract_last, preferred_element_type=jnp.float32
            )
            expped = jnp.exp(scores)
            inverse = 1.0 / jnp.sum(expped, axis=0, keepdims=True)
            inv_ref[step, pl.ds(number, 1), :] = inverse
            probs = (expped * inverse).astype(jnp.bfloat16)
            att_t[h, :] = jnp.dot(vt[h, :], probs, preferred_element_type=jnp.float32)
        att_ref[rows, :] = att_t[...].T.astype(jnp.bfloat16)


def attend(joined, text_kv, qk_gain):
    tokens, width = joined.shape[0], joined.shape[1] // 3
    text = text_kv.shape[1]
    chunk = 256 if tokens % 256 == 0 else tokens
    keys = tokens + text
    bf16 = jnp.bfloat16
    whole = pl.BlockSpec(memory_space=pltpu.VMEM)
    return pl.pallas_call(
        attend_kernel,
        out_shape=(
            jax.ShapeDtypeStruct((tokens, width), bf16),
            jax.ShapeDtypeStruct((tokens, width), bf16),
            jax.ShapeDtypeStruct((keys, width), bf16),
            jax.ShapeDtypeStruct((keys, width), bf16),
            jax.ShapeDtypeStruct((tokens // chunk, width // HEAD_DIM, chunk), jnp.float32),
        ),
        in_specs=[whole] * 3,
        out_specs=(whole,) * 5,
        scratch_shapes=[pltpu.VMEM((width, keys), bf16), pltpu.VMEM((width, chunk), jnp.float32)],
        compiler_params=pltpu.CompilerParams(vmem_limit_bytes=VMEM_LIMIT),
        name="attend",
    )(joined, text_kv, qk_gain)


def norm_back(x, gain, grad):
    rounded = grad.astype(jnp.bfloat16).astype(jnp.float32) * gain
    scale = lax.rsqrt(jnp.mean(x * x, axis=-1, keepdims=True) + epsilon)
    along = jnp.mean(rounded * x, axis=-1, keepdims=True)
    return scale * (rounded - x * (scale * scale * along))


def attend_back_kernel(
    joined_ref, q_ref, k_ref, v_ref, inv_ref, g_ref, gain_ref, out_ref, kt, grad_k, grad_v, grad_q
):
    tokens, width = q_ref.shape
    chunk = inv_ref.shape[2]
    gain_q, gain_k = gain_ref[0:1], gain_ref[1:2]
    kt[...] = k_ref[...].astype(jnp.float32).T.astype(jnp.bfloat16)
    grad_k[...] = jnp.zeros_like(grad_k)
    grad_v[...] = jnp.zeros_like(grad_v)

    @pl.loop(0, tokens // chunk)
    def _(step):
        rows = pl.ds(pl.multiple_of(step * chunk, chunk), chunk)
        for number, h in enumerate(per_head(width)):
            query, grad = q_ref[rows, h], g_ref[rows, h]
            scores = lax.dot_general(
                k_ref[:, h], query, contract_last, preferred_element_type=jnp.float32
            )
            probs = jnp.exp(scores) * inv_ref[step, pl.ds(number, 1), :]
            grad_probs = lax.dot_general(
                v_ref[:, h], grad, contract_last, preferred_element_type=jnp.float32
            )
            centre = jnp.sum(probs * grad_probs, axis=0, keepdims=True)
            grad_logits = (probs * (grad_probs - centre)).astype(jnp.bfloat16)
            grad_v[:, h] += jnp.dot(
                probs[:tokens].astype(jnp.bfloat16), grad, preferred_element_type=jnp.float32
            )
            grad_k[:, h] += jnp.dot(
                grad_logits[:tokens], query, preferred_element_type=jnp.float32
            )
            grad_q[h, :] = jnp.dot(kt[h, :], grad_logits, preferred_element_type=jnp.float32)
        back = grad_q[...].T * SCALE
        out_ref[rows, :width] = jnp.concatenate(
            [norm_back(joined_ref[rows, h], gain_q, back[:, h]) for h in per_head(width)], axis=1
        ).astype(jnp.bfloat16)

    @pl.loop(0, tokens // chunk)
    def _(step):
        rows = pl.ds(pl.multiple_of(step * chunk, chunk), chunk)
        part = joined_ref[rows, width : 2 * width]
        back = grad_k[rows, :]
        out_ref[rows, width : 2 * width] = jnp.concatenate(
            [norm_back(part[:, h], gain_k, back[:, h]) for h in per_head(width)], axis=1
        ).astype(jnp.bfloat16)
        out_ref[rows, 2 * width :] = grad_v[rows, :].astype(jnp.bfloat16)


def attend_back(joined, q, k, v, inverse, grad_heads, qk_gain):
    tokens, width = q.shape
    chunk = inverse.shape[2]
    whole = pl.BlockSpec(memory_space=pltpu.VMEM)
    return pl.pallas_call(
        attend_back_kernel,
        out_shape=jax.ShapeDtypeStruct((tokens, 3 * width), jnp.bfloat16),
        in_specs=[whole] * 7,
        out_specs=whole,
        scratch_shapes=[
            pltpu.VMEM((width, k.shape[0]), jnp.bfloat16),
            pltpu.VMEM((tokens, width), jnp.float32),
            pltpu.VMEM((tokens, width), jnp.float32),
            pltpu.VMEM((width, chunk), jnp.float32),
        ],
        compiler_params=pltpu.CompilerParams(vmem_limit_bytes=VMEM_LIMIT),
        name="attend_back",
    )(joined, q, k, v, inverse, grad_heads, qk_gain)


def reduce_kernel(
    sizes, lat_ref, ada_ref, lat_out, ada_out,
    pair_lat, pair_ada, sum_lat, sum_ada, seq_lat, seq_ada, tot_lat, tot_ada,
    part_lat, part_ada, rep_lat, rep_ada, gathered,
    pair_sems, seq_sems, rep_sems, last_sems,
):
    seqs, chips = sizes
    s, r = lax.axis_index("seq"), lax.axis_index("rep")
    z, c = r // 2, lax.rem(r, 2)
    other = 1 - c
    sibling = {"rep": 2 * z + other}
    seq_peers = [lax.rem(s + k, seqs) for k in range(seqs)]
    rep_peers = [lax.rem(z + k, chips) for k in range(chips)]

    barrier = pltpu.get_barrier_semaphore()
    peers = (
        [sibling]
        + [{"seq": p} for p in seq_peers[1:]]
        + [{"rep": 2 * p + c} for p in rep_peers[1:]]
    )
    for peer in peers:
        pl.semaphore_signal(barrier, inc=1, device_id=peer, device_id_type=MESH)
    pl.semaphore_wait(barrier, len(peers))

    def send(source, target, sems, index, peer):
        copy = pltpu.make_async_remote_copy(
            src_ref=source, dst_ref=target, send_sem=sems.at[0, index], recv_sem=sems.at[1, index],
            device_id=peer, device_id_type=MESH,
        )
        copy.start()
        return copy

    order = list(range(1, seqs)) + [0]
    pair_copies = {}
    for k in order:
        to = seq_peers[k]
        pair_copies[k] = (
            send(lat_ref.at[other, to], pair_lat.at[k], pair_sems, 2 * k, sibling),
            send(ada_ref.at[other, to], pair_ada.at[k], pair_sems, 2 * k + 1, sibling),
        )
    f32, bf16 = jnp.float32, jnp.bfloat16
    seq_copies = []
    for k in order:
        to = seq_peers[k]
        for copy in pair_copies[k]:
            copy.wait_recv()
        if k:
            for i in range(chips):
                sum_lat[k - 1, i] = (
                    lat_ref[c, to, i].astype(f32) + pair_lat[k, i].astype(f32)
                ).astype(bf16)
                sum_ada[k - 1, i] = (
                    ada_ref[c, to, i].astype(f32) + pair_ada[k, i].astype(f32)
                ).astype(bf16)
            seq_copies.append(
                send(sum_lat.at[k - 1], seq_lat.at[k - 1], seq_sems, 2 * k - 2, {"seq": to})
            )
            seq_copies.append(
                send(sum_ada.at[k - 1], seq_ada.at[k - 1], seq_sems, 2 * k - 1, {"seq": to})
            )
        else:
            for i in range(chips):
                tot_lat[i] = lat_ref[c, to, i].astype(f32) + pair_lat[k, i].astype(f32)
                tot_ada[i] = ada_ref[c, to, i].astype(f32) + pair_ada[k, i].astype(f32)
    for copy in seq_copies:
        copy.wait_recv()
    rep_copies = []
    for j in list(range(1, chips)) + [0]:
        to = rep_peers[j]
        lat, ada = tot_lat[to], tot_ada[to]
        for k in range(seqs - 1):
            lat += seq_lat[k, to].astype(f32)
            ada += seq_ada[k, to].astype(f32)
        if j:
            part_lat[j - 1] = lat.astype(bf16)
            part_ada[j - 1] = ada.astype(bf16)
            peer = {"rep": 2 * to + c}
            rep_copies.append(
                send(part_ada.at[j - 1], rep_ada.at[j - 1], rep_sems, 2 * j - 1, peer)
            )
            rep_copies.append(
                send(part_lat.at[j - 1], rep_lat.at[j - 1], rep_sems, 2 * j - 2, peer)
            )
        else:
            lat_out[...] = lat
            tot_ada[0] = ada
    for copy in rep_copies:
        copy.wait_recv()
    ada = tot_ada[0]
    for j in range(chips - 1):
        ada += rep_ada[j].astype(f32)
    gathered[s] = ada.astype(bf16)
    last_copies = []
    for k in range(1, seqs):
        last_copies.append(
            send(gathered.at[s], gathered.at[s], last_sems, k - 1, {"seq": seq_peers[k]})
        )
    lat = lat_out[...]
    for j in range(chips - 1):
        lat += rep_lat[j].astype(f32)
    lat_out[...] = lat
    for k in range(1, seqs):
        source = lax.rem(s - k + seqs, seqs)
        pltpu.make_async_remote_copy(
            src_ref=gathered.at[s], dst_ref=gathered.at[source], send_sem=last_sems.at[0, k - 1],
            recv_sem=last_sems.at[1, k - 1], device_id={"seq": source}, device_id_type=MESH,
        ).wait_recv()
    ada_out[...] = gathered[...].astype(f32)
    for copy in [one for pair in pair_copies.values() for one in pair] + seq_copies + rep_copies + last_copies:
        copy.wait_send()


def reduce_all(lat, ada):
    _, seqs, chips, rows, width = lat.shape
    a_rows, lanes = ada.shape[3:]
    bf16, f32 = jnp.bfloat16, jnp.float32
    whole = pl.BlockSpec(memory_space=pltpu.VMEM)

    def both(lead, kind=bf16):
        return [pltpu.VMEM(lead + (rows, width), kind), pltpu.VMEM(lead + (a_rows, lanes), kind)]

    sems = lambda count: pltpu.SemaphoreType.DMA((2, count))
    return pl.pallas_call(
        functools.partial(reduce_kernel, (seqs, chips)),
        out_shape=(
            jax.ShapeDtypeStruct((rows, width), f32),
            jax.ShapeDtypeStruct((seqs, a_rows, lanes), f32),
        ),
        in_specs=[whole] * 2,
        out_specs=(whole,) * 2,
        scratch_shapes=both((seqs, chips)) + both((seqs - 1, chips)) + both((seqs - 1, chips))
        + both((chips,), f32) + both((chips - 1,)) + both((chips - 1,))
        + [pltpu.VMEM((seqs, a_rows, lanes), bf16)]
        + [sems(2 * seqs), sems(2 * seqs - 2), sems(2 * chips - 2), sems(seqs - 1)],
        compiler_params=pltpu.CompilerParams(
            collective_id=0, has_side_effects=True, vmem_limit_bytes=VMEM_LIMIT
        ),
        name="reduce_all",
    )(lat, ada)


def shards(
    latent, noise, timestep, text_kv, qk_gain, prompt,
    w_qkv, a_qkv, b_qkv, w_out, a_out, b_out, w_patch,
):
    seqs, reps = lax.axis_size("seq"), lax.axis_size("rep")
    chips = reps // 2
    s = lax.axis_index("seq")
    bf16, f32 = jnp.bfloat16, jnp.float32
    rank = a_qkv.shape[1]
    inner = w_qkv.shape[1] // 3
    width = inner // seqs

    def my_columns(weight):
        parts = weight.reshape(weight.shape[0], 3, inner)
        return lax.dynamic_slice_in_dim(parts, s * width, width, 2).reshape(-1, 3 * width)

    w_in = lax.all_gather(my_columns(w_qkv), "rep", axis=0, tiled=True)
    b_in = my_columns(b_qkv)
    latent_rows = lax.all_gather(latent, "rep", axis=0, tiled=True)
    noise_level = timestep[0].astype(f32) / 1000.0
    mixed_in = (1.0 - noise_level) * latent_rows.astype(f32) + noise_level * noise[0].astype(f32)
    centred = mixed_in - jnp.mean(mixed_in, axis=-1, keepdims=True)
    deviation = lax.rsqrt(jnp.mean(centred * centred, axis=-1, keepdims=True) + epsilon)
    normed = lax.all_gather((centred * deviation).astype(bf16), "seq", axis=0, tiled=True)
    deviation = lax.all_gather(deviation, "seq", axis=0, tiled=True)
    w_in, normed, w_out = lax.optimization_barrier((w_in, normed, w_out))
    w_back = lax.all_gather(w_out, "rep", axis=0, tiled=True)

    low_rank = jnp.dot(normed, a_qkv, preferred_element_type=f32).astype(bf16)
    joined = jnp.dot(normed, w_in, preferred_element_type=f32) + jnp.dot(
        low_rank, b_in, preferred_element_type=f32
    )
    attended_heads, q, k, v, inverse = attend(joined, text_kv, qk_gain)
    attended = lax.all_to_all(attended_heads, "seq", split_axis=0, concat_axis=1, tiled=True)
    low_out, patch_pre, partial_sum = project_out(
        attended, mixed_in, noise_level, w_back, a_out, b_out, w_patch
    )
    pooled = lax.psum(partial_sum, "seq") / (latent_rows.shape[0] * seqs)
    score_value, grad_pooled = jax.value_and_grad(reward)(pooled, prompt)
    grad_denoised, grad_attended, grad_a_out, grad_b_out = backward_out(
        patch_pre, grad_pooled, noise_level, attended, low_out, w_back, a_out, b_out, w_patch
    )
    grad_heads = lax.all_to_all(grad_attended, "seq", split_axis=1, concat_axis=0, tiled=True)
    grad_joined = attend_back(joined, q, k, v, inverse, grad_heads, qk_gain)

    grad_low = lax.dot_general(
        grad_joined, b_in, contract_last, preferred_element_type=f32
    ).astype(bf16)
    grad_normed = lax.dot_general(
        grad_joined, w_in, contract_last, preferred_element_type=f32
    ) + lax.dot_general(grad_low, a_qkv, contract_last, preferred_element_type=f32)
    normed32 = normed.astype(f32)
    grad_mixed = deviation * (
        grad_normed
        - jnp.mean(grad_normed, axis=-1, keepdims=True)
        - normed32 * jnp.mean(grad_normed * normed32, axis=-1, keepdims=True)
    )
    tokens, model = grad_mixed.shape
    rows = tokens // seqs
    mine = (lax.broadcasted_iota(jnp.int32, (seqs, 1, 1), 0) == s).astype(f32)
    grad_mixed = grad_mixed.reshape(seqs, rows, model) + mine * grad_denoised[None]
    lat = ((1.0 - noise_level) * grad_mixed).astype(bf16)
    lat = lat.reshape(seqs, chips, 2, rows // reps, model).transpose(2, 0, 1, 3, 4)

    grad_a_qkv = lax.dot_general(normed, grad_low, contract_first, preferred_element_type=f32)
    grad_b_qkv = lax.dot_general(grad_joined, low_rank, contract_first, preferred_element_type=f32)
    spread = jnp.zeros((3, seqs, width, rank), bf16)
    spread = lax.dynamic_update_slice(
        spread, grad_b_qkv.astype(bf16).reshape(3, 1, width, rank), (0, s, 0, 0)
    )
    by_rep = [
        grad_a_qkv.astype(bf16).reshape(reps, -1, rank),
        spread.reshape(reps, -1, rank),
        grad_a_out.astype(bf16).reshape(reps, -1, rank),
        grad_b_out.astype(bf16).reshape(reps, -1, rank),
    ]
    lengths = [one.shape[1] for one in by_rep]
    ada = jnp.concatenate(by_rep, axis=1)
    half = ada.shape[1] // 2
    ada = jnp.concatenate([ada[:, :half], ada[:, half:]], axis=2)
    ada = ada.reshape(chips, 2, seqs, half // seqs, 2 * rank).transpose(1, 2, 0, 3, 4)
    latent_grad, ada = reduce_all(lat, ada)
    ada = ada.reshape(half, 2 * rank)
    ada = jnp.concatenate([ada[:, :rank], ada[:, rank:]], axis=0)
    pieces, at = [], 0
    for length in lengths:
        pieces.append(ada[at : at + length])
        at += length
    return (
        score_value.reshape(1), latent_grad, pieces[0], pieces[1].T, pieces[2], pieces[3].T,
    )


def solution(mesh):
    in_specs = (
        P(("seq", "rep"), None),
        P("rep", "seq", None),
        P("rep"),
        P(None, None, "seq"),
        P(),
        P(),
        P("rep", None),
        P(),
        P(),
        P("rep", None),
        P(),
        P(),
        P(),
    )
    out_specs = (
        P("rep"),
        P(("seq", "rep"), None),
        P("rep", None),
        P(None, "rep"),
        P("rep", None),
        P(None, "rep"),
    )
    return jax.shard_map(shards, mesh=mesh, in_specs=in_specs, out_specs=out_specs, check_vma=False)
```

time: 749 us -> 405 us (0.54)
  waiting for transfers between devices: 405 us -> 144 us
  Pallas kernels: 0 us -> 92.2 us
  matrix products: 132 us -> 56.3 us
  local copies, waits for them, and re-layouts: 100 us -> 32.8 us
  other arithmetic: 44.5 us -> 14 us
  starting transfers between devices: 18.5 us -> 7.42 us
  blocking collectives: 27 us -> 34.8 us
    pallas_call x0 -> x3, Pallas kernels: none -> 92.2 us  [the longest x1 53 us: reduce_all(): pl.pallas_call(functools.partial(reduce_kernel, (seqs, chips)), out_shape...]
    unnamed x14 -> x3, waiting for transfers between devices: 83.3 us -> 0.05 us
    psum x2 -> x0, waiting for transfers between devices: 80.1 us -> none  [the longest x1 40.3 us: shards(): lax.psum(shard_b_qkv.astype(jnp.bfloat16), 'seq').astype(jnp.float32)]
    dot_general x51 -> x9, matrix products: 103 us -> 29.3 us  [the longest x1 8.4 us: shards(): lax.dot_general(grad_joined, w_in, contract_last, preferred_element_type=...]
    all_gather x2 -> x3, waiting for transfers between devices: 179 us -> 129 us  [the longest x1 60.7 us: shards(): w_in = lax.all_gather(my_columns(w_qkv), 'rep', axis=0, tiled=True)]
    all_to_all x2 -> x0, waiting for transfers between devices: 47.5 us -> none  [the longest x1 31.9 us: shards(): lax.all_to_all(stacked, 'seq', split_axis=2, concat_axis=0, tiled=True)]
    slice x8 -> x3, local copies, waits for them, and re-layouts: 18.2 us -> 0.31 us  [the longest x1 0.17 us: shards(): ada = jnp.concatenate([ada[:, :rank], ada[:, rank:]], axis=0)]
    convert_element_type x15 -> x2, other arithmetic: 16.9 us -> 1.43 us  [the longest x1 1.43 us: shards(): (centred * deviation).astype(bf16)]
  transfers between devices with their start and end apart: 13 -> 5, of which waited for: 11 -> 5; matrix products, arithmetic and copies ran while one was open for 24% -> 7% of each run, Pallas kernels for 0% -> 4%
where the time goes in v1:
time: 405 us; the launch traced here: 400 us
  waiting for transfers between devices  144 us (36%)
  Pallas kernels  92.2 us (23%)
  matrix products  56.3 us (14%)
  blocking collectives  34.8 us (9%)
  local copies, waits for them, and re-layouts  32.8 us (8%)
  between operations  19.2 us (5%)
  other arithmetic  14 us (3%)
  starting transfers between devices  7.42 us (2%)
    all_gather x1, waiting for transfers between devices, shards(): w_in = lax.all_gather(my_columns(w_qkv), 'rep', axis=0, tiled=True)  60.7 us
    pallas_call x1, Pallas kernels, reduce_all(): pl.pallas_call(functools.partial(reduce_kernel, (seqs, chips)), out_shape...  53 us
    all_gather x1, waiting for transfers between devices, shards(): lax.all_gather((centred * deviation).astype(bf16), 'seq', axis=0, tiled=T...  38.6 us
    all_gather x1, waiting for transfers between devices, shards(): w_back = lax.all_gather(w_out, 'rep', axis=0, tiled=True)  29.5 us
    pallas_call x1, Pallas kernels, attend_back(): pl.pallas_call(attend_back_kernel, out_shape=jax.ShapeDtypeStruct((tokens...  22.3 us
    all_gather x1, blocking collectives, shards(): latent_rows = lax.all_gather(latent, 'rep', axis=0, tiled=True)  17.9 us
    pallas_call x1, Pallas kernels, attend(): pl.pallas_call(attend_kernel, out_shape=(jax.ShapeDtypeStruct((tokens, wi...  16.9 us
    psum x1, blocking collectives, shards(): pooled = lax.psum(partial_sum, 'seq') / (latent_rows.shape[0] * seqs)  16.9 us
  transfers between devices with their start and end apart: 5, of which 5 were waited for; matrix products, arithmetic and copies ran while one was open for 7% of the time, Pallas kernels for 4%

profile of v1, /device:TPU:0, one launch (start us, length us, event | category | flops | bytes accessed | tf_op | source)
XLA Modules:
  0.0 400.3 jit_solution(15609292622208970521)
XLA Ops:
  8.0 17.9 %all_gather.15 = bf16[192,2432]{1,0:T(8,128)(2,1)S(1)} all-gather(bf16[24,2432]{1,0:T(8,128)(2,1)} %param.13), channel_id=1, replica_groups=mesh['rep'=8,'seq'=4] {'rep'}, dimensions={0}, use_global_device_ids=true | all-gather | bytes 1050624 | tf_op jit(solution)/shard_map/all_gather | solution.py:375
  25.9 1.6 fusion.22
  27.5 0.6 multiply_reduce_fusion
  28.1 0.6 dynamic-slice
  29.4 0.6 broadcast.81
  30.0 1.4 fusion.40
  31.3 1.4 multiply_convert_fusion.1
  32.8 9.0 %reshape.108 = bf16[304,3,1536]{2,1,0:T(4,128)(2,1)} reshape(bf16[304,4608]{1,0:T(8,128)(2,1)} %param.19) | data formatting | bytes 5603328 | tf_op jit(solution)/shard_map/reshape | solution.py:370
  41.8 1.6 constant_dynamic-slice_fusion.1
  43.5 1.0 copy.53
  44.4 0.2 all-gather.9.cloned.1.call-start
  44.7 38.6 %all-gather.7.cloned.1.call-done = bf16[768,2432]{1,0:T(8,128)(2,1)} async-done(((bf16[192,2432]{1,0:T(8,128)(2,1)}), bf16[768,2432]{1,0:T(8,128)(2,1)}) %all-gather.7.cloned.1.call-update) | async-done | bytes 3735568 | tf_op jit(solution)/shard_map/all_gather | solution.py:380
  83.2 60.7 %all-gather.5.cloned.1.call-done = bf16[2432,1152]{1,0:T(8,128)(2,1)} async-done(((bf16[304,1152]{1,0:T(8,128)(2,1)}), bf16[2432,1152]{1,0:T(8,128)(2,1)}) %all-gather.5.cloned.1.call-update) | async-done | bytes 5603344 | tf_op jit(solution)/shard_map/all_gather | solution.py:373
  144.0 0.4 reshape.110
  144.6 3.4 convolution_convert_fusion.5
  148.0 7.8 %fusion.43 = f32[768,1152]{1,0:T(8,128)S(1)} fusion(bf16[768,2432]{1,0:T(8,128)(2,1)S(1)} %copy-done.1, bf16[2432,1152]{1,0:T(8,128)(2,1)} %all-gather.5.cloned.1.call-done), kind=kOutput, calls=%fused_computation.81 | convolution fusion | flops 4303355904 | bytes 12877824 | tf_op jit(solution)/shard_map/dot_general | solution.py:386
  155.9 2.4 convolution_add_fusion.1.joined_ref
  158.3 16.9 %attend.1 = (bf16[768,384]{1,0:T(8,128)(2,1)}, bf16[768,384]{1,0:T(8,128)(2,1)}, bf16[896,384]{1,0:T(8,128)(2,1)}, bf16[896,384]{1,0:T(8,128)(2,1)}, f32[3,6,256]{2,1,0:T(8,128)}) custom-call(f32[768,1152]{1,0:T(8,128)} %convolution_add_fusion.1.joined_ref, bf16[2,128,384]{2,1,0:T(8,128)(2,1)} %text_ref.1, f32[2,64]{1,0:T(2,128)} %gain_ref.3), custom_call_target="tpu_custom_call" | custom-call | tf_op jit(solution)/shard_map/attend/pallas_call | solution.py:125
  175.2 3.6 all-to-all-start
  178.8 9.2 %all-to-all-done = bf16[4,192,384]{2,1,0:T(8,128)(2,1)S(1)} async-done(((bf16[4,192,384]{2,1,0:T(8,128)(2,1)}), bf16[4,192,384]{2,1,0:T(8,128)(2,1)S(1)}, u32[]{:S(2)}, u32[]{:S(2)}) %all-to-all-start) | async-done | bytes 589856 | tf_op jit(solution)/shard_map/all_to_all | solution.py:390
  188.1 1.2 convolution_convert_fusion.7
  189.4 29.5 %all-gather.9.cloned.1.call-done = bf16[1536,2432]{1,0:T(8,128)(2,1)} async-done(((bf16[192,2432]{1,0:T(8,128)(2,1)}), bf16[1536,2432]{1,0:T(8,128)(2,1)}) %all-gather.9.cloned.1.call-update) | async-done | bytes 7471120 | tf_op jit(solution)/shard_map/all_gather | solution.py:383
  218.8 6.1 %fusion.44 = f32[192,2432]{1,0:T(8,128)} fusion(bf16[192,1536]{1,0:T(8,128)(2,1)S(1)} %bitcast.91, bf16[1536,2432]{1,0:T(8,128)(2,1)} %all-gather.9.cloned.1.call-done), kind=kOutput, calls=%fused_computation.82 | convolution fusion | flops 1434451968 | bytes 9928704 | tf_op jit(solution)/shard_map/dot_general | solution.py:21
  225.0 6.1 %fusion.20 = (f32[1280]{0:T(1024)S(1)}, f32[192,1280]{1,0:T(8,128)}) fusion(bf16[2432,1280]{1,0:T(8,128)(2,1)} %param.25, f32[192,2432]{1,0:T(8,128)} %fusion.44, bf16[192,64]{0,1:T(8,128)(2,1)S(1)} %convolution_convert_fusion.7, bf16[64,2432]{1,0:T(8,128)(2,1)S(1)} %copy-done.11, f32[]{:T(128)} %bitcast, bf16[1,192,2432]{2,1,0:T(8,128)(2,1)S(1)} %copy-done.4, ...), kind=kOutput, calls=%fused_computation.44 | convolution fusion | flops 1261558528 | bytes 11285512 | tf_op jit(solution)/shard_map/dot_general | solution.py:25
  231.1 16.9 %all-reduce.1 = (f32[1280]{0:T(1024)S(1)}, f32[768]{0:T(1024)S(1)}) all-reduce(f32[1280]{0:T(1024)S(1)} %get-tuple-element.53, f32[768]{0:T(1024)} %get-tuple-element.51), channel_id=1, replica_groups=mesh['rep'=8,'seq'=4] {'seq'}, use_global_device_ids=true, to_apply=%region_3.0 | all-reduce | flops 2048 | bytes 16384 | tf_op jit(solution)/shard_map/psum | solution.py:394
  247.9 0.6 multiply_reduce_fusion.1
  250.6 6.8 %multiply_convert_fusion = (bf16[192,2432]{1,0:T(8,128)(2,1)S(1)}, f32[192,2432]{1,0:T(8,128)}) fusion(f32[]{:T(128)S(6)} %neg.3, bf16[2432,1280]{1,0:T(8,128)(2,1)} %param.25, f32[192,1280]{1,0:T(8,128)} %get-tuple-element.54, f32[1280]{0:T(1024)S(1)} %get-tuple-element.46, f32[1280]{0:T(1024)S(1)} %get-tuple-element.45), kind=kOutput, calls=%fused_computation.22 | convolution fusion | flops 1200979968 | bytes 10020868 | tf_op jit(solution)/shard_map/dot_general | solution.py:43
  257.4 0.4 convolution_convert_fusion.6
  257.8 5.7 %fusion.45 = f32[192,1536]{1,0:T(8,128)S(1)} fusion(bf16[192,2432]{1,0:T(8,128)(2,1)S(1)} %get-tuple-element.55, bf16[1536,2432]{1,0:T(8,128)(2,1)} %all-gather.9.cloned.1.call-done), kind=kOutput, calls=%fused_computation.83 | convolution fusion | flops 1434451968 | bytes 9584640 | tf_op jit(solution)/shard_map/dot_general | solution.py:51
  263.6 0.3 fusion.9
  263.9 0.9 copy.67
  264.8 3.5 all-to-all-start.1
  268.3 0.2 convolution_convert_fusion.2
  268.5 0.2 reshape.117
  268.8 0.3 convolution_convert_fusion
  269.1 0.5 reshape.118
  269.5 5.7 %all-to-all-done.1 = bf16[192,4,384]{2,0,1:T(8,128)(2,1)S(1)} async-done(((bf16[192,4,384]{2,0,1:T(8,128)(2,1)}), bf16[192,4,384]{2,0,1:T(8,128)(2,1)S(1)}, u32[]{:S(2)}, u32[]{:S(2)}) %all-to-all-start.1) | async-done | bytes 589856 | tf_op jit(solution)/shard_map/all_to_all | solution.py:399
  275.2 0.8 copy-done.5
  276.1 22.3 %attend_back.1 = bf16[768,1152]{1,0:T(8,128)(2,1)} custom-call(f32[768,1152]{1,0:T(8,128)} %convolution_add_fusion.1.joined_ref, bf16[768,384]{1,0:T(8,128)(2,1)} %get-tuple-element.20.q_ref, bf16[896,384]{1,0:T(8,128)(2,1)} %get-tuple-element.21.k_ref, bf16[896,384]{1,0:T(8,128)(2,1)} %get-tuple-element.22.v_ref, f32[3,6,256]{2,1,0:T(8,128)} %get-tuple-element.23.inv_ref, ...), custom_call_target="tpu_custom_call" | custom-call | tf_op jit(solution)/shard_map/attend_back/pallas_call | solution.py:200
  298.3 8.4 %fusion.46 = f32[768,2432]{1,0:T(8,128)S(1)} fusion(bf16[768,1152]{1,0:T(8,128)(2,1)} %attend_back.1, bf16[2432,1152]{1,0:T(8,128)(2,1)} %all-gather.5.cloned.1.call-done), kind=kOutput, calls=%fused_computation.84 | convolution fusion | flops 4303355904 | bytes 14843904 | tf_op jit(solution)/shard_map/dot_general | solution.py:405
  306.8 0.6 convolution_convert_fusion.4
  307.4 0.4 convolution_convert_fusion.3
  307.8 1.0 copy-done.2
  308.8 0.8 convolution_convert_fusion.1
  309.6 5.1 %fusion.41 = (f32[768]{0:T(1024)S(1)}, f32[768]{0:T(1024)S(1)}, f32[768,2432]{1,0:T(8,128)}) fusion(bf16[768,2432]{1,0:T(8,128)(2,1)S(1)} %copy-done.2, f32[768,2432]{1,0:T(8,128)S(1)} %fusion.46, bf16[768,64]{0,1:T(8,128)(2,1)S(1)} %convolution_convert_fusion.4, bf16[2432,64]{0,1:T(8,128)(2,1)S(1)} %copy-done), kind=kOutput, calls=%fused_computation.79 | convolution fusion | flops 248412672 | bytes 19093504 | tf_op jit(solution)/shard_map/dot_general | solution.py:407
  314.8 0.2 broadcast_in_dim.8
  314.9 2.9 dynamic_update_slice.3
  317.8 0.7 reshape.116
  318.6 0.5 reshape.114
  319.0 1.6 concatenate.14
  320.7 0.3 fusion.10
  321.0 2.2 copy.45
  323.2 2.6 copy.66
  325.9 5.2 %fusion.2 = f32[768,2432]{1,0:T(8,128)S(1)} fusion(bf16[768,2432]{1,0:T(8,128)(2,1)} %all-gather.7.cloned.1.call-done, f32[768,2432]{1,0:T(8,128)} %get-tuple-element.57, f32[768]{0:T(1024)S(1)} %get-tuple-element.44, f32[768]{0:T(1024)S(1)} %get-tuple-element.58, f32[768]{0:T(1024)S(1)} %get-tuple-element.59), kind=kLoop, calls=%fused_computation.4 | loop fusion | flops 9338880 | bytes 18686976 | tf_op jit(solution)/shard_map/mul | solution.py:409
  331.1 2.9 fusion.8.lat_ref
  334.0 53.0 %reduce_all.1 = (f32[24,2432]{1,0:T(8,128)}, f32[4,172,128]{2,1,0:T(8,128)}) custom-call(bf16[2,4,4,24,2432]{4,3,2,1,0:T(8,128)(2,1)} %fusion.8.lat_ref, bf16[2,4,4,172,128]{4,3,2,1,0:T(8,128)(2,1)} %bitcast.88), custom_call_target="tpu_custom_call" | custom-call | tf_op jit(solution)/shard_map/reduce_all/pallas_call | solution.py:338
  387.0 1.1 reshape.120
  388.1 0.1 slice_bitcast_fusion
  388.2 0.2 fusion.42
  388.5 0.8 copy.47
  389.2 0.8 copy.48
  390.1 0.7 copy.49
  390.8 0.8 copy.50
  391.5 0.7 copy.72
  (44 shorter events, 0.6 us)
Async XLA Ops:
  7.2 137.4 %copy-start = (bf16[2432,64]{0,1:T(8,128)(2,1)S(1)}, bf16[2432,64]{0,1:T(8,128)(2,1)}, u32[]{:S(2)}) copy-start(bf16[2432,64]{0,1:T(8,128)(2,1)} %param.20) | copy-start | bytes 933892
  7.2 20.9 %copy-start.14 = (u32[32]{0:T(128)S(1)}, u32[32]{0:T(128)}, u32[]{:S(2)}) copy-start(u32[32]{0:T(128)} %constant.55) | copy-start | bytes 388
  7.2 20.3 %copy-start.4 = (bf16[1,192,2432]{2,1,0:T(8,128)(2,1)S(1)}, bf16[1,192,2432]{2,1,0:T(8,128)(2,1)}, u32[]{:S(2)}) copy-start(bf16[1,192,2432]{2,1,0:T(8,128)(2,1)} %param.14) | copy-start | bytes 2801668
  7.2 76.0 %all-gather.7.cloned.1.call-start = ((), (), s32[]{:S(2)}) async-start(), calls=%async_computation.3 | async-start | bytes 4669440 | tf_op jit(solution)/shard_map/all_gather | solution.py:380
  32.8 111.2 %all-gather.5.cloned.1.call-start = ((), (), s32[]{:S(2)}) async-start(), calls=%async_computation.2 | async-start | bytes 6303744 | tf_op jit(solution)/shard_map/all_gather | solution.py:373
  41.8 102.2 %copy-start.10 = (bf16[64,4608]{1,0:T(8,128)(2,1)S(1)}, bf16[64,4608]{1,0:T(8,128)(2,1)}, u32[]{:S(2)}) copy-start(bf16[64,4608]{1,0:T(8,128)(2,1)} %param.21) | copy-start | bytes 1769476
  44.4 174.4 %all-gather.9.cloned.1.call-start = ((), (), s32[]{:S(2)}) async-start(), calls=%async_computation.4 | async-start | bytes 8404992 | tf_op jit(solution)/shard_map/all_gather | solution.py:383
  144.6 3.5 copy-start.1
  148.0 7.9 %copy-start.7 = (bf16[768,64]{0,1:T(8,128)(2,1)}, bf16[768,64]{0,1:T(8,128)(2,1)S(1)}, u32[]{:S(2)}) copy-start(bf16[768,64]{0,1:T(8,128)(2,1)S(1)} %convolution_convert_fusion.5) | copy-start | bytes 294916
  175.2 12.9 %all-to-all-start = ((bf16[4,192,384]{2,1,0:T(8,128)(2,1)}), bf16[4,192,384]{2,1,0:T(8,128)(2,1)S(1)}, u32[]{:S(2)}, u32[]{:S(2)}) async-start(bf16[4,192,384]{2,1,0:T(8,128)(2,1)} %bitcast.102), calls=%async_computation | async-start | bytes 1179648 | tf_op jit(solution)/shard_map/all_to_all | solution.py:390
  189.3 35.6 %copy-start.11 = (bf16[64,2432]{1,0:T(8,128)(2,1)S(1)}, bf16[64,2432]{1,0:T(8,128)(2,1)}, u32[]{:S(2)}) copy-start(bf16[64,2432]{1,0:T(8,128)(2,1)} %param.24) | copy-start | bytes 933892
  225.0 23.0 %copy-start.13 = (f32[1280]{0:T(1024)S(1)}, f32[1280]{0:T(1024)}, u32[]{:S(2)}) copy-start(f32[1280]{0:T(1024)} %param.18) | copy-start | bytes 15364
  257.8 5.8 %copy-start.9 = (bf16[1536,64]{0,1:T(8,128)(2,1)S(1)}, bf16[1536,64]{0,1:T(8,128)(2,1)}, u32[]{:S(2)}) copy-start(bf16[1536,64]{0,1:T(8,128)(2,1)} %param.23) | copy-start | bytes 589828
  264.8 10.4 %all-to-all-start.1 = ((bf16[192,4,384]{2,0,1:T(8,128)(2,1)}), bf16[192,4,384]{2,0,1:T(8,128)(2,1)S(1)}, u32[]{:S(2)}, u32[]{:S(2)}) async-start(bf16[192,4,384]{2,0,1:T(8,128)(2,1)} %bitcast.86), calls=%async_computation.1 | async-start | bytes 1179648 | tf_op jit(solution)/shard_map/all_to_all | solution.py:399
  275.2 0.8 copy-start.5
  298.3 8.4 %copy-start.3 = (bf16[768,1152]{1,0:T(8,128)(2,1)S(1)}, bf16[768,1152]{1,0:T(8,128)(2,1)}, u32[]{:S(2)}) copy-start(bf16[768,1152]{1,0:T(8,128)(2,1)} %attend_back.1) | copy-start | bytes 5308420
  298.3 9.1 %copy-start.8 = (bf16[768,64]{0,1:T(8,128)(2,1)S(1)}, bf16[768,64]{0,1:T(8,128)(2,1)}, u32[]{:S(2)}) copy-start(bf16[768,64]{0,1:T(8,128)(2,1)} %copy-done.7) | copy-start | bytes 294916
  306.7 2.1 copy-start.2
  325.9 5.2 %copy-start.6 = (f32[192,2432]{1,0:T(8,128)S(1)}, f32[192,2432]{1,0:T(8,128)}, u32[]{:S(2)}) copy-start(f32[192,2432]{1,0:T(8,128)} %get-tuple-element.56) | copy-start | bytes 5603332
  387.0 4.5 %copy-start.12 = (f32[24,2432]{1,0:T(8,128)S(1)}, f32[24,2432]{1,0:T(8,128)}, u32[]{:S(2)}) copy-start(f32[24,2432]{1,0:T(8,128)} %get-tuple-element.67) | copy-start | bytes 700420
Sparse Core Ops, SparseCore 0:
  32.9 50.3 all-gather.6
  84.9 59.0 all-gather.4
  145.6 73.1 all-gather.8

commit v2 on v1

--- a/solution.py
+++ b/solution.py
@@ -354,6 +354,127 @@
     )(lat, ada)
 
 
+def gather_kernel(
+    sizes, level_ref, lat_ref, noise_ref, w_ref,
+    w_out_ref, normed_ref, dev_ref, mixed_ref,
+    lat_all, lat_rows, own_sem, lat_sems, w_sems, norm_sems, dev_sems,
+):
+    seqs, chips = sizes
+    s, r = lax.axis_index("seq"), lax.axis_index("rep")
+    z, c = r // 2, lax.rem(r, 2)
+    sibling = {"rep": 2 * z + 1 - c}
+    ahead = [lax.rem(z + j, chips) for j in range(chips)]
+    behind = [lax.rem(z - j + chips, chips) for j in range(chips)]
+    seq_ahead = [lax.rem(s + k, seqs) for k in range(seqs)]
+    seq_behind = [lax.rem(s - k + seqs, seqs) for k in range(seqs)]
+    f32, bf16 = jnp.float32, jnp.bfloat16
+
+    barrier = pltpu.get_barrier_semaphore()
+    peers = (
+        [sibling]
+        + [{"seq": p} for p in seq_ahead[1:]]
+        + [{"rep": 2 * p + c} for p in ahead[1:]]
+    )
+    for peer in peers:
+        pl.semaphore_signal(barrier, inc=1, device_id=peer, device_id_type=MESH)
+    pl.semaphore_wait(barrier, len(peers))
+
+    def copy(source, target, sems, index, peer):
+        return pltpu.make_async_remote_copy(
+            src_ref=source, dst_ref=target, send_sem=sems.at[0, index], recv_sem=sems.at[1, index],
+            device_id=peer, device_id_type=MESH,
+        )
+
+    started = []
+
+    def send(*args):
+        one = copy(*args)
+        one.start()
+        started.append(one)
+
+    for source, target, sems in ((lat_ref, lat_all, lat_sems), (w_ref, w_out_ref, w_sems)):
+        for j in range(1, chips):
+            send(source, target.at[r], sems, j, {"rep": 2 * ahead[j] + c})
+        send(source, target.at[r], sems, chips, sibling)
+    own = pltpu.make_async_copy(w_ref, w_out_ref.at[r], own_sem)
+    own.start()
+    lat_all[r] = lat_ref[...]
+
+    def forward(target, sems):
+        for j in range(1, chips):
+            block = target.at[2 * behind[j] + c]
+            copy(block, block, sems, j, sibling).wait_recv()
+            send(block, block, sems, chips + j, sibling)
+
+    def arrive(target, sems):
+        for j in range(chips):
+            block = target.at[2 * behind[j] + 1 - c]
+            copy(block, block, sems, chips + j, sibling).wait_recv()
+
+    forward(lat_all, lat_sems)
+    arrive(lat_all, lat_sems)
+    length = lat_ref.shape[0]
+    rows = noise_ref.shape[0]
+    for i in range(2 * chips):
+        lat_rows[i * length : (i + 1) * length, :] = lat_all[i].astype(f32)
+    level = level_ref[0:1, 0:1]
+    chunk = 32 if rows % 32 == 0 else rows
+
+    @pl.loop(0, rows // chunk)
+    def _(step):
+        at = pl.ds(pl.multiple_of(step * chunk, chunk), chunk)
+        mixed = (1.0 - level) * lat_rows[at, :] + level * noise_ref[at, :].astype(f32)
+        mixed_ref[at, :] = mixed
+        centred = mixed - jnp.mean(mixed, axis=-1, keepdims=True)
+        deviation = lax.rsqrt(jnp.mean(centred * centred, axis=-1, keepdims=True) + epsilon)
+        normed_ref[s, at, :] = (centred * deviation).astype(bf16)
+        dev_ref[s, at, :] = jnp.broadcast_to(deviation, (chunk, dev_ref.shape[2]))
+
+    for k in range(1, seqs):
+        send(normed_ref.at[s], normed_ref.at[s], norm_sems, k - 1, {"seq": seq_ahead[k]})
+        send(dev_ref.at[s], dev_ref.at[s], dev_sems, k - 1, {"seq": seq_ahead[k]})
+    forward(w_out_ref, w_sems)
+    own.wait()
+    for k in range(1, seqs):
+        for target, sems in ((normed_ref, norm_sems), (dev_ref, dev_sems)):
+            block = target.at[seq_behind[k]]
+            copy(block, block, sems, k - 1, {"seq": seq_ahead[k]}).wait_recv()
+    arrive(w_out_ref, w_sems)
+    for one in started:
+        one.wait_send()
+
+
+def gather_all(level, latent, noise, weight):
+    seqs, reps = lax.axis_size("seq"), lax.axis_size("rep")
+    chips = reps // 2
+    rows, model = noise.shape
+    bf16, f32 = jnp.bfloat16, jnp.float32
+    whole = pl.BlockSpec(memory_space=pltpu.VMEM)
+    sems = lambda count: pltpu.SemaphoreType.DMA((2, count))
+    return pl.pallas_call(
+        functools.partial(gather_kernel, (seqs, chips)),
+        out_shape=(
+            jax.ShapeDtypeStruct((reps,) + weight.shape, bf16),
+            jax.ShapeDtypeStruct((seqs, rows, model), bf16),
+            jax.ShapeDtypeStruct((seqs, rows, 128), f32),
+            jax.ShapeDtypeStruct((rows, model), f32),
+        ),
+        in_specs=[whole] * 4,
+        out_specs=(whole,) * 4,
+        scratch_shapes=[
+            pltpu.VMEM((reps,) + latent.shape, bf16),
+            pltpu.VMEM((rows, model), f32),
+            pltpu.SemaphoreType.DMA,
+            sems(2 * chips), sems(2 * chips), sems(seqs - 1), sems(seqs - 1),
+        ],
+        compiler_params=pltpu.CompilerParams(
+            collective_id=1, has_side_effects=True, vmem_limit_bytes=VMEM_LIMIT
+        ),
+        cost_estimate=pl.CostEstimate(flops=10**10, bytes_accessed=2 * 10**8, transcendentals=0),
+        name="gather_all",
+    )(level, latent, noise, weight)
+
+
 def shards(
     latent, noise, timestep, text_kv, qk_gain, prompt,
     w_qkv, a_qkv, b_qkv, w_out, a_out, b_out, w_patch,
@@ -367,20 +488,23 @@
     width = inner // seqs
 
     def my_columns(weight):
-        parts = weight.reshape(weight.shape[0], 3, inner)
-        return lax.dynamic_slice_in_dim(parts, s * width, width, 2).reshape(-1, 3 * width)
-
-    w_in = lax.all_gather(my_columns(w_qkv), "rep", axis=0, tiled=True)
+        return jnp.concatenate(
+            [
+                lax.dynamic_slice_in_dim(weight, part * inner + s * width, width, 1)
+                for part in range(3)
+            ],
+            axis=1,
+        )
+
+    w_back = lax.all_gather(w_out, "rep", axis=0, tiled=True)
     b_in = my_columns(b_qkv)
-    latent_rows = lax.all_gather(latent, "rep", axis=0, tiled=True)
     noise_level = timestep[0].astype(f32) / 1000.0
-    mixed_in = (1.0 - noise_level) * latent_rows.astype(f32) + noise_level * noise[0].astype(f32)
-    centred = mixed_in - jnp.mean(mixed_in, axis=-1, keepdims=True)
-    deviation = lax.rsqrt(jnp.mean(centred * centred, axis=-1, keepdims=True) + epsilon)
-    normed = lax.all_gather((centred * deviation).astype(bf16), "seq", axis=0, tiled=True)
-    deviation = lax.all_gather(deviation, "seq", axis=0, tiled=True)
-    w_in, normed, w_out = lax.optimization_barrier((w_in, normed, w_out))
-    w_back = lax.all_gather(w_out, "rep", axis=0, tiled=True)
+    w_in, normed, deviation, mixed_in = gather_all(
+        jnp.full((1, 128), noise_level), latent, noise[0], my_columns(w_qkv)
+    )
+    w_in = w_in.reshape(-1, 3 * width)
+    normed = normed.reshape(-1, normed.shape[2])
+    deviation = deviation.reshape(-1, deviation.shape[2])[:, :1]
 
     low_rank = jnp.dot(normed, a_qkv, preferred_element_type=f32).astype(bf16)
     joined = jnp.dot(normed, w_in, preferred_element_type=f32) + jnp.dot(
@@ -391,7 +515,7 @@
     low_out, patch_pre, partial_sum = project_out(
         attended, mixed_in, noise_level, w_back, a_out, b_out, w_patch
     )
-    pooled = lax.psum(partial_sum, "seq") / (latent_rows.shape[0] * seqs)
+    pooled = lax.psum(partial_sum, "seq") / normed.shape[0]
     score_value, grad_pooled = jax.value_and_grad(reward)(pooled, prompt)
     grad_denoised, grad_attended, grad_a_out, grad_b_out = backward_out(
         patch_pre, grad_pooled, noise_level, attended, low_out, w_back, a_out, b_out, w_patch

time: 405 us -> 380 us (0.938)
  Pallas kernels: 92.2 us -> 237 us
  waiting for transfers between devices: 144 us -> 15.3 us
  blocking collectives: 34.8 us -> 9 us
  local copies, waits for them, and re-layouts: 32.8 us -> 20.7 us
  matrix products: 56.3 us -> 63.3 us
  other arithmetic: 14 us -> 7.63 us
    pallas_call x0 -> x1, Pallas kernels: none -> 117 us  [gather_all(): pl.pallas_call(functools.partial(gather_kernel, (seqs, chips)), out_shape...]
    all_gather x2 -> x0, waiting for transfers between devices: 99.3 us -> none  [the longest x1 60.7 us: shards(): w_in = lax.all_gather(my_columns(w_qkv), 'rep', axis=0, tiled=True)]
    all_gather x1, waiting for transfers between devices: 29.5 us -> 0.02 us  [shards(): w_back = lax.all_gather(w_out, 'rep', axis=0, tiled=True)]
    pallas_call x1, Pallas kernels: 53 us -> 80.3 us  [reduce_all(): pl.pallas_call(functools.partial(reduce_kernel, (seqs, chips)), out_shape...]
    all_gather x1 -> x0, blocking collectives: 17.9 us -> none  [shards(): latent_rows = lax.all_gather(latent, 'rep', axis=0, tiled=True)]
    reshape x2 -> x0, local copies, waits for them, and re-layouts: 9.43 us -> none  [my_columns(): parts = weight.reshape(weight.shape[0], 3, inner)]
    psum x1, blocking collectives: 16.9 us -> 9 us  [shards(): pooled = lax.psum(partial_sum, 'seq') / normed.shape[0]]
  transfers between devices with their start and end apart: 5 -> 3, of which waited for: 5 -> 2; matrix products, arithmetic and copies ran while one was open for 7% -> 5% of each run, Pallas kernels for 4% -> 35%
where the time goes in v2:
time: 380 us; the launch traced here: 378 us
  Pallas kernels  237 us (62%)
  matrix products  63.3 us (17%)
  local copies, waits for them, and re-layouts  20.7 us (5%)
  between operations  18.3 us (5%)
  waiting for transfers between devices  15.3 us (4%)
  blocking collectives  9 us (2%)
  other arithmetic  7.63 us (2%)
  starting transfers between devices  7.39 us (2%)
    pallas_call x1, Pallas kernels, gather_all(): pl.pallas_call(functools.partial(gather_kernel, (seqs, chips)), out_shape...  117 us
    pallas_call x1, Pallas kernels, reduce_all(): pl.pallas_call(functools.partial(reduce_kernel, (seqs, chips)), out_shape...  80.3 us
    pallas_call x1, Pallas kernels, attend_back(): pl.pallas_call(attend_back_kernel, out_shape=jax.ShapeDtypeStruct((tokens...  22.3 us
    pallas_call x1, Pallas kernels, attend(): pl.pallas_call(attend_kernel, out_shape=(jax.ShapeDtypeStruct((tokens, wi...  16.9 us
    dot_general x1, matrix products, shards(): lax.dot_general(grad_joined, w_in, contract_last, preferred_element_type=...  9.91 us
    all_to_all x1, waiting for transfers between devices, shards(): lax.all_to_all(attended_heads, 'seq', split_axis=0, concat_axis=1, tiled=...  9.08 us
    psum x1, blocking collectives, shards(): pooled = lax.psum(partial_sum, 'seq') / normed.shape[0]  9 us
    dot_general x1, matrix products, shards(): jnp.dot(normed, w_in, preferred_element_type=f32)  7.81 us
  transfers between devices with their start and end apart: 3, of which 2 were waited for; matrix products, arithmetic and copies ran while one was open for 5% of the time, Pallas kernels for 35%

profile of v2, /device:TPU:0, one launch (start us, length us, event | category | flops | bytes accessed | tf_op | source)
XLA Modules:
  0.0 378.3 jit_solution(17931321559856524611)
XLA Ops:
  7.2 0.0 copy-start
  7.2 0.0 all-gather.2.cloned.1.call-start
  7.2 0.7 all-gather.2.cloned.1.call-update
  8.6 0.9 constant_dynamic-slice_fusion.2
  9.4 0.0 copy-start.9
  9.5 0.0 copy-start.11
  9.5 1.3 constant_dynamic-slice_fusion.5
  10.8 0.9 pad_maximum_fusion.1.w_ref
  11.7 0.5 broadcast_in_dim.16.level_ref
  12.2 117.2 %gather_all.1 = (bf16[8,304,1152]{2,1,0:T(8,128)(2,1)}, bf16[4,192,2432]{2,1,0:T(8,128)(2,1)}, f32[4,192,128]{2,1,0:T(8,128)}, f32[192,2432]{1,0:T(8,128)}) custom-call(f32[1,128]{1,0:T(1,128)} %broadcast_in_dim.16.level_ref, bf16[24,2432]{1,0:T(8,128)(2,1)} %lat_ref.1, bf16[192,2432]{1,0:T(8,128)(2,1)} %bitcast.88, bf16[304,1152]{1,0:T(8,128)(2,1)} %pad_maximum_fusion.1.w_ref), custom_call_target="tpu_custom_call" | custom-call | flops 10000000000 | bytes 200000000 | tf_op jit(solution)/shard_map/gather_all/pallas_call | solution.py:454
  129.5 3.5 convolution_convert_fusion.5
  133.0 7.8 %fusion.43 = f32[768,1152]{1,0:T(8,128)S(1)} fusion(bf16[768,2432]{1,0:T(8,128)(2,1)S(1)} %bitcast.75, bf16[2432,1152]{1,0:T(8,128)(2,1)} %bitcast.89), kind=kOutput, calls=%fused_computation.83 | convolution fusion | flops 4303355904 | bytes 12877824 | tf_op jit(solution)/shard_map/dot_general | solution.py:510
  140.8 2.4 convolution_add_fusion.1.joined_ref
  143.3 16.9 %attend.1 = (bf16[768,384]{1,0:T(8,128)(2,1)}, bf16[768,384]{1,0:T(8,128)(2,1)}, bf16[896,384]{1,0:T(8,128)(2,1)}, bf16[896,384]{1,0:T(8,128)(2,1)}, f32[3,6,256]{2,1,0:T(8,128)}) custom-call(f32[768,1152]{1,0:T(8,128)} %convolution_add_fusion.1.joined_ref, bf16[2,128,384]{2,1,0:T(8,128)(2,1)} %text_ref.1, f32[2,64]{1,0:T(2,128)} %gain_ref.3), custom_call_target="tpu_custom_call" | custom-call | tf_op jit(solution)/shard_map/attend/pallas_call | solution.py:125
  160.1 3.7 all-to-all-start
  163.8 0.2 slice_reduce_fusion
  164.0 9.1 %all-to-all-done = bf16[4,192,384]{2,1,0:T(8,128)(2,1)S(1)} async-done(((bf16[4,192,384]{2,1,0:T(8,128)(2,1)}), bf16[4,192,384]{2,1,0:T(8,128)(2,1)S(1)}, u32[]{:S(2)}, u32[]{:S(2)}) %all-to-all-start) | async-done | bytes 589856 | tf_op jit(solution)/shard_map/all_to_all | solution.py:514
  173.1 0.1 copy.56
  173.2 0.3 convolution_convert_fusion.7
  173.5 0.0 all-gather.2.cloned.1.call-done
  173.5 6.2 %fusion.44 = f32[192,2432]{1,0:T(8,128)} fusion(bf16[192,1536]{1,0:T(8,128)(2,1)S(1)} %bitcast.80, bf16[1536,2432]{1,0:T(8,128)(2,1)} %all-gather.2.cloned.1.call-done), kind=kOutput, calls=%fused_computation.84 | convolution fusion | flops 1434451968 | bytes 9928704 | tf_op jit(solution)/shard_map/dot_general | solution.py:21
  179.8 6.1 %fusion.20 = (f32[1280]{0:T(1024)S(1)}, f32[192,1280]{1,0:T(8,128)}) fusion(bf16[2432,1280]{1,0:T(8,128)(2,1)} %param.25, f32[192,2432]{1,0:T(8,128)S(1)} %copy-done.5, f32[192,2432]{1,0:T(8,128)} %fusion.44, bf16[192,64]{0,1:T(8,128)(2,1)S(1)} %convolution_convert_fusion.7, bf16[64,2432]{1,0:T(8,128)(2,1)S(1)} %copy-done.7, f32[]{:T(128)} %bitcast), kind=kOutput, calls=%fused_computation.41 | convolution fusion | flops 1259223808 | bytes 11285508 | tf_op jit(solution)/shard_map/dot_general | solution.py:25
  185.9 9.0 %psum.7 = f32[1280]{0:T(1024)S(1)} all-reduce(f32[1280]{0:T(1024)S(1)} %get-tuple-element.57), channel_id=1, replica_groups=mesh['rep'=8,'seq'=4] {'seq'}, use_global_device_ids=true, to_apply=%region_1.0 | all-reduce | flops 1280 | bytes 10240 | tf_op jit(solution)/shard_map/psum | solution.py:518
  194.9 0.7 multiply_reduce_fusion
  197.7 6.7 %multiply_convert_fusion = (bf16[192,2432]{1,0:T(8,128)(2,1)S(1)}, f32[192,2432]{1,0:T(8,128)}) fusion(f32[]{:T(128)S(6)} %neg.3, bf16[2432,1280]{1,0:T(8,128)(2,1)} %param.25, f32[192,1280]{1,0:T(8,128)} %get-tuple-element.58, f32[1280]{0:T(1024)S(1)} %get-tuple-element.46, f32[1280]{0:T(1024)S(1)} %get-tuple-element.45), kind=kOutput, calls=%fused_computation.21 | convolution fusion | flops 1200979968 | bytes 10020868 | tf_op jit(solution)/shard_map/dot_general | solution.py:43
  204.4 0.4 convolution_convert_fusion.6
  204.8 5.7 %fusion.45 = f32[192,1536]{1,0:T(8,128)S(1)} fusion(bf16[192,2432]{1,0:T(8,128)(2,1)S(1)} %get-tuple-element.59, bf16[1536,2432]{1,0:T(8,128)(2,1)} %all-gather.2.cloned.1.call-done), kind=kOutput, calls=%fused_computation.85 | convolution fusion | flops 1434451968 | bytes 9584640 | tf_op jit(solution)/shard_map/dot_general | solution.py:51
  210.6 0.3 fusion.9
  210.9 0.9 copy.69
  211.8 3.7 all-to-all-start.1
  215.5 0.3 convolution_convert_fusion
  215.8 0.5 reshape.86
  216.3 0.2 convolution_convert_fusion.2
  216.5 0.2 reshape.85
  216.8 5.5 %all-to-all-done.1 = bf16[192,4,384]{2,0,1:T(8,128)(2,1)S(1)} async-done(((bf16[192,4,384]{2,0,1:T(8,128)(2,1)}), bf16[192,4,384]{2,0,1:T(8,128)(2,1)S(1)}, u32[]{:S(2)}, u32[]{:S(2)}) %all-to-all-start.1) | async-done | bytes 589856 | tf_op jit(solution)/shard_map/all_to_all | solution.py:523
  222.2 0.8 copy-done.4
  223.1 22.3 %attend_back.1 = bf16[768,1152]{1,0:T(8,128)(2,1)} custom-call(f32[768,1152]{1,0:T(8,128)} %convolution_add_fusion.1.joined_ref, bf16[768,384]{1,0:T(8,128)(2,1)} %get-tuple-element.22.q_ref, bf16[896,384]{1,0:T(8,128)(2,1)} %get-tuple-element.23.k_ref, bf16[896,384]{1,0:T(8,128)(2,1)} %get-tuple-element.24.v_ref, f32[3,6,256]{2,1,0:T(8,128)} %get-tuple-element.25.inv_ref, ...), custom_call_target="tpu_custom_call" | custom-call | tf_op jit(solution)/shard_map/attend_back/pallas_call | solution.py:200
  245.3 2.0 convolution_convert_fusion.3
  247.4 2.1 convolution_convert_fusion.4
  249.5 9.9 %fusion.46 = f32[768,2432]{1,0:T(8,128)} fusion(bf16[768,1152]{1,0:T(8,128)(2,1)S(1)} %copy-done.3, bf16[2432,1152]{1,0:T(8,128)(2,1)} %bitcast.90), kind=kOutput, calls=%fused_computation.86 | convolution fusion | flops 4303355904 | bytes 14843904 | tf_op jit(solution)/shard_map/dot_general | solution.py:529
  259.4 0.1 reshape.89
  259.5 0.2 broadcast_in_dim.19
  259.7 2.9 dynamic_update_slice.3
  262.5 0.7 reshape.84
  263.3 1.8 concatenate.22
  265.1 0.1 slice.42
  265.2 2.8 convolution_convert_fusion.1
  268.0 1.2 reshape.82
  269.2 1.3 fusion.10
  270.5 1.9 copy.47
  272.5 1.3 copy.68
  273.8 6.4 %fusion.41 = (f32[768]{0:T(1024)S(1)}, f32[768]{0:T(1024)S(1)}, f32[768,2432]{1,0:T(8,128)S(1)}) fusion(bf16[4,192,2432]{2,1,0:T(8,128)(2,1)} %get-tuple-element.18, f32[768,2432]{1,0:T(8,128)} %fusion.46, bf16[768,64]{0,1:T(8,128)(2,1)S(1)} %convolution_convert_fusion.4, bf16[2432,64]{0,1:T(8,128)(2,1)S(1)} %copy-done), kind=kOutput, calls=%fused_computation.81 | convolution fusion | flops 248412672 | bytes 19093504 | tf_op jit(solution)/shard_map/dot_general | solution.py:531
  280.2 1.8 fusion.2
  282.0 2.9 fusion.8.lat_ref
  284.9 80.3 %reduce_all.1 = (f32[24,2432]{1,0:T(8,128)}, f32[4,172,128]{2,1,0:T(8,128)}) custom-call(bf16[2,4,4,24,2432]{4,3,2,1,0:T(8,128)(2,1)} %fusion.8.lat_ref, bf16[2,4,4,172,128]{4,3,2,1,0:T(8,128)(2,1)} %bitcast.77), custom_call_target="tpu_custom_call" | custom-call | tf_op jit(solution)/shard_map/reduce_all/pallas_call | solution.py:338
  365.1 1.1 reshape.88
  366.2 0.2 fusion.42
  366.4 0.1 slice_bitcast_fusion
  366.5 0.1 slice.46
  366.6 0.8 copy.50
  367.4 0.8 copy.49
  368.2 0.8 copy.52
  368.9 0.7 copy.51
  369.7 0.7 copy.73
  (40 shorter events, 0.1 us)
Async XLA Ops:
  7.2 122.3 %copy-start = (bf16[2432,64]{0,1:T(8,128)(2,1)S(1)}, bf16[2432,64]{0,1:T(8,128)(2,1)}, u32[]{:S(2)}) copy-start(bf16[2432,64]{0,1:T(8,128)(2,1)} %param.20) | copy-start | bytes 933892
  7.2 166.3 %all-gather.2.cloned.1.call-start = ((), (), s32[]{:S(2)}) async-start(), calls=%async_computation.2 | async-start | bytes 8404992 | tf_op jit(solution)/shard_map/all_gather | solution.py:499
  9.4 131.4 %copy-start.9 = (bf16[64,384]{1,0:T(8,128)(2,1)}, bf16[64,384]{1,0:T(8,128)(2,1)S(1)}, u32[]{:S(2)}) copy-start(bf16[64,384]{1,0:T(8,128)(2,1)S(1)} %get-tuple-element.50) | copy-start | bytes 147460
  9.5 131.4 %copy-start.11 = (bf16[64,384]{1,0:T(8,128)(2,1)}, bf16[64,384]{1,0:T(8,128)(2,1)S(1)}, u32[]{:S(2)}) copy-start(bf16[64,384]{1,0:T(8,128)(2,1)S(1)} %get-tuple-element.51) | copy-start | bytes 147460
  9.5 131.3 %copy-start.13 = (bf16[64,384]{1,0:T(8,128)(2,1)}, bf16[64,384]{1,0:T(8,128)(2,1)S(1)}, u32[]{:S(2)}) copy-start(bf16[64,384]{1,0:T(8,128)(2,1)S(1)} %get-tuple-element.52) | copy-start | bytes 147460
  129.5 3.5 copy-start.1
  143.3 20.6 %copy-start.15 = (f32[4,192,128]{2,1,0:T(8,128)S(1)}, f32[4,192,128]{2,1,0:T(8,128)}, u32[]{:S(2)}) copy-start(f32[4,192,128]{2,1,0:T(8,128)} %get-tuple-element.21) | copy-start | bytes 1179652
  143.3 29.9 %copy-start.8 = (bf16[1536,64]{0,1:T(8,128)(2,1)S(1)}, bf16[1536,64]{0,1:T(8,128)(2,1)}, u32[]{:S(2)}) copy-start(bf16[1536,64]{0,1:T(8,128)(2,1)} %param.23) | copy-start | bytes 589828
  160.1 12.9 %all-to-all-start = ((bf16[4,192,384]{2,1,0:T(8,128)(2,1)}), bf16[4,192,384]{2,1,0:T(8,128)(2,1)S(1)}, u32[]{:S(2)}, u32[]{:S(2)}) async-start(bf16[4,192,384]{2,1,0:T(8,128)(2,1)} %bitcast.86), calls=%async_computation | async-start | bytes 1179648 | tf_op jit(solution)/shard_map/all_to_all | solution.py:514
  173.5 6.3 %copy-start.16 = (bf16[192,64]{0,1:T(8,128)(2,1)}, bf16[192,64]{0,1:T(8,128)(2,1)S(1)}, u32[]{:S(2)}) copy-start(bf16[192,64]{0,1:T(8,128)(2,1)S(1)} %convolution_convert_fusion.7) | copy-start | bytes 73732
  173.5 6.3 %copy-start.5 = (f32[192,2432]{1,0:T(8,128)S(1)}, f32[192,2432]{1,0:T(8,128)}, u32[]{:S(2)}) copy-start(f32[192,2432]{1,0:T(8,128)} %get-tuple-element.17) | copy-start | bytes 5603332
  173.5 6.3 %copy-start.7 = (bf16[64,2432]{1,0:T(8,128)(2,1)S(1)}, bf16[64,2432]{1,0:T(8,128)(2,1)}, u32[]{:S(2)}) copy-start(bf16[64,2432]{1,0:T(8,128)(2,1)} %param.24) | copy-start | bytes 933892
  179.8 15.2 %copy-start.19 = (f32[1280]{0:T(1024)S(1)}, f32[1280]{0:T(1024)}, u32[]{:S(2)}) copy-start(f32[1280]{0:T(1024)} %param.18) | copy-start | bytes 15364
  210.5 5.0 %copy-start.17 = (bf16[192,64]{0,1:T(8,128)(2,1)S(1)}, bf16[192,64]{0,1:T(8,128)(2,1)}, u32[]{:S(2)}) copy-start(bf16[192,64]{0,1:T(8,128)(2,1)} %copy-done.16) | copy-start | bytes 73732
  211.8 10.4 %all-to-all-start.1 = ((bf16[192,4,384]{2,0,1:T(8,128)(2,1)}), bf16[192,4,384]{2,0,1:T(8,128)(2,1)S(1)}, u32[]{:S(2)}, u32[]{:S(2)}) async-start(bf16[192,4,384]{2,0,1:T(8,128)(2,1)} %bitcast.72), calls=%async_computation.1 | async-start | bytes 1179648 | tf_op jit(solution)/shard_map/all_to_all | solution.py:523
  222.2 0.8 copy-start.4
  223.1 24.3 %copy-start.10 = (bf16[64,384]{1,0:T(8,128)(2,1)S(1)}, bf16[64,384]{1,0:T(8,128)(2,1)}, u32[]{:S(2)}) copy-start(bf16[64,384]{1,0:T(8,128)(2,1)} %copy-done.9) | copy-start | bytes 147460
  223.1 24.3 %copy-start.12 = (bf16[64,384]{1,0:T(8,128)(2,1)S(1)}, bf16[64,384]{1,0:T(8,128)(2,1)}, u32[]{:S(2)}) copy-start(bf16[64,384]{1,0:T(8,128)(2,1)} %copy-done.11) | copy-start | bytes 147460
  223.1 24.3 %copy-start.14 = (bf16[64,384]{1,0:T(8,128)(2,1)S(1)}, bf16[64,384]{1,0:T(8,128)(2,1)}, u32[]{:S(2)}) copy-start(bf16[64,384]{1,0:T(8,128)(2,1)} %copy-done.13) | copy-start | bytes 147460
  245.3 4.2 %copy-start.3 = (bf16[768,1152]{1,0:T(8,128)(2,1)S(1)}, bf16[768,1152]{1,0:T(8,128)(2,1)}, u32[]{:S(2)}) copy-start(bf16[768,1152]{1,0:T(8,128)(2,1)} %attend_back.1) | copy-start | bytes 5308420
  273.8 6.4 %copy-start.2 = (bf16[4,192,2432]{2,1,0:T(8,128)(2,1)S(1)}, bf16[4,192,2432]{2,1,0:T(8,128)(2,1)}, u32[]{:S(2)}) copy-start(bf16[4,192,2432]{2,1,0:T(8,128)(2,1)} %get-tuple-element.18) | copy-start | bytes 11206660
  280.2 1.8 copy-start.6
  365.1 4.5 %copy-start.18 = (f32[24,2432]{1,0:T(8,128)S(1)}, f32[24,2432]{1,0:T(8,128)}, u32[]{:S(2)}) copy-start(f32[24,2432]{1,0:T(8,128)} %get-tuple-element.71) | copy-start | bytes 700420
Sparse Core Ops, SparseCore 0:
  9.7 138.6 all-gather.1

commit v3 on v2

--- a/solution.py
+++ b/solution.py
@@ -496,7 +496,10 @@
             axis=1,
         )
 
-    w_back = lax.all_gather(w_out, "rep", axis=0, tiled=True)
+    share = w_out.shape[0] // seqs
+    w_back = lax.all_gather(
+        lax.dynamic_slice_in_dim(w_out, s * share, share, 0), ("rep", "seq"), axis=0, tiled=True
+    )
     b_in = my_columns(b_qkv)
     noise_level = timestep[0].astype(f32) / 1000.0
     w_in, normed, deviation, mixed_in = gather_all(

time: 380 us -> 365 us (0.961)
  Pallas kernels: 237 us -> 217 us
  local copies, waits for them, and re-layouts: 20.7 us -> 24.7 us
    pallas_call x1, Pallas kernels: 117 us -> 84.8 us  [gather_all(): pl.pallas_call(functools.partial(gather_kernel, (seqs, chips)), out_shape...]
    pallas_call x1, Pallas kernels: 80.3 us -> 93.4 us  [reduce_all(): pl.pallas_call(functools.partial(reduce_kernel, (seqs, chips)), out_shape...]
  transfers between devices with their start and end apart: 3 -> 3, of which waited for: 2 -> 2; matrix products, arithmetic and copies ran while one was open for 5% -> 5% of each run, Pallas kernels for 35% -> 28%
where the time goes in v3:
time: 365 us; the launch traced here: 362 us
  Pallas kernels  217 us (59%)
  matrix products  63.2 us (17%)
  local copies, waits for them, and re-layouts  24.7 us (7%)
  between operations  18.3 us (5%)
  waiting for transfers between devices  14.8 us (4%)
  blocking collectives  9.01 us (2%)
  other arithmetic  7.57 us (2%)
  starting transfers between devices  7.39 us (2%)
    pallas_call x1, Pallas kernels, reduce_all(): pl.pallas_call(functools.partial(reduce_kernel, (seqs, chips)), out_shape...  93.4 us
    pallas_call x1, Pallas kernels, gather_all(): pl.pallas_call(functools.partial(gather_kernel, (seqs, chips)), out_shape...  84.8 us
    pallas_call x1, Pallas kernels, attend_back(): pl.pallas_call(attend_back_kernel, out_shape=jax.ShapeDtypeStruct((tokens...  22.3 us
    pallas_call x1, Pallas kernels, attend(): pl.pallas_call(attend_kernel, out_shape=(jax.ShapeDtypeStruct((tokens, wi...  16.9 us
    dot_general x1, matrix products, shards(): lax.dot_general(grad_joined, w_in, contract_last, preferred_element_type=...  9.91 us
    all_to_all x1, waiting for transfers between devices, shards(): lax.all_to_all(attended_heads, 'seq', split_axis=0, concat_axis=1, tiled=...  9.26 us
    psum x1, blocking collectives, shards(): pooled = lax.psum(partial_sum, 'seq') / normed.shape[0]  9.01 us
    dot_general x1, matrix products, shards(): jnp.dot(normed, w_in, preferred_element_type=f32)  7.81 us
  transfers between devices with their start and end apart: 3, of which 2 were waited for; matrix products, arithmetic and copies ran while one was open for 5% of the time, Pallas kernels for 28%

profile of v3, /device:TPU:0, one launch (start us, length us, event | category | flops | bytes accessed | tf_op | source)
XLA Modules:
  0.0 362.4 jit_solution(6299365591292885664)
XLA Ops:
  7.2 0.0 all-gather.2.cloned.1.call-start
  7.2 1.1 copy-done
  8.4 0.7 constant_dynamic-slice_fusion
  9.1 0.0 all-gather.2.cloned.1.call-update
  9.7 0.9 constant_dynamic-slice_fusion.3
  10.6 1.3 constant_dynamic-slice_fusion.6
  11.9 0.9 pad_maximum_fusion.1.w_ref
  12.8 0.5 broadcast_in_dim.16.level_ref
  13.3 84.8 %gather_all.1 = (bf16[8,304,1152]{2,1,0:T(8,128)(2,1)}, bf16[4,192,2432]{2,1,0:T(8,128)(2,1)}, f32[4,192,128]{2,1,0:T(8,128)}, f32[192,2432]{1,0:T(8,128)}) custom-call(f32[1,128]{1,0:T(1,128)} %broadcast_in_dim.16.level_ref, bf16[24,2432]{1,0:T(8,128)(2,1)} %lat_ref.1, bf16[192,2432]{1,0:T(8,128)(2,1)} %bitcast.88, bf16[304,1152]{1,0:T(8,128)(2,1)} %pad_maximum_fusion.1.w_ref), custom_call_target="tpu_custom_call" | custom-call | flops 10000000000 | bytes 200000000 | tf_op jit(solution)/shard_map/gather_all/pallas_call | solution.py:454
  98.2 3.4 convolution_convert_fusion.5
  101.6 0.5 copy-done.2
  102.1 7.8 %fusion.43 = f32[768,1152]{1,0:T(8,128)S(1)} fusion(bf16[768,2432]{1,0:T(8,128)(2,1)S(1)} %bitcast.75, bf16[2432,1152]{1,0:T(8,128)(2,1)} %bitcast.89), kind=kOutput, calls=%fused_computation.84 | convolution fusion | flops 4303355904 | bytes 12877824 | tf_op jit(solution)/shard_map/dot_general | solution.py:513
  110.0 2.4 convolution_add_fusion.1.joined_ref
  112.4 16.9 %attend.1 = (bf16[768,384]{1,0:T(8,128)(2,1)}, bf16[768,384]{1,0:T(8,128)(2,1)}, bf16[896,384]{1,0:T(8,128)(2,1)}, bf16[896,384]{1,0:T(8,128)(2,1)}, f32[3,6,256]{2,1,0:T(8,128)}) custom-call(f32[768,1152]{1,0:T(8,128)} %convolution_add_fusion.1.joined_ref, bf16[2,128,384]{2,1,0:T(8,128)(2,1)} %text_ref.1, f32[2,64]{1,0:T(2,128)} %gain_ref.3), custom_call_target="tpu_custom_call" | custom-call | tf_op jit(solution)/shard_map/attend/pallas_call | solution.py:125
  129.3 3.7 %all-to-all-start = ((bf16[4,192,384]{2,1,0:T(8,128)(2,1)}), bf16[4,192,384]{2,1,0:T(8,128)(2,1)S(1)}, u32[]{:S(2)}, u32[]{:S(2)}) async-start(bf16[4,192,384]{2,1,0:T(8,128)(2,1)} %bitcast.86), calls=%async_computation | async-start | bytes 1179648 | tf_op jit(solution)/shard_map/all_to_all | solution.py:517
  133.0 0.2 slice_reduce_fusion
  133.1 9.3 %all-to-all-done = bf16[4,192,384]{2,1,0:T(8,128)(2,1)S(1)} async-done(((bf16[4,192,384]{2,1,0:T(8,128)(2,1)}), bf16[4,192,384]{2,1,0:T(8,128)(2,1)S(1)}, u32[]{:S(2)}, u32[]{:S(2)}) %all-to-all-start) | async-done | bytes 589856 | tf_op jit(solution)/shard_map/all_to_all | solution.py:517
  142.4 0.1 copy.56
  142.5 0.3 convolution_convert_fusion.7
  142.8 0.0 all-gather.2.cloned.1.call-done
  142.8 6.2 %fusion.44 = f32[192,2432]{1,0:T(8,128)} fusion(bf16[192,1536]{1,0:T(8,128)(2,1)S(1)} %bitcast.80, bf16[1536,2432]{1,0:T(8,128)(2,1)} %all-gather.2.cloned.1.call-done), kind=kOutput, calls=%fused_computation.85 | convolution fusion | flops 1434451968 | bytes 9928704 | tf_op jit(solution)/shard_map/dot_general | solution.py:21
  149.1 6.1 %fusion.20 = (f32[1280]{0:T(1024)S(1)}, f32[192,1280]{1,0:T(8,128)}) fusion(bf16[2432,1280]{1,0:T(8,128)(2,1)} %param.25, f32[192,2432]{1,0:T(8,128)S(1)} %copy-done.6, f32[192,2432]{1,0:T(8,128)} %fusion.44, bf16[192,64]{0,1:T(8,128)(2,1)S(1)} %convolution_convert_fusion.7, bf16[64,2432]{1,0:T(8,128)(2,1)S(1)} %copy-done.10, f32[]{:T(128)} %bitcast), kind=kOutput, calls=%fused_computation.41 | convolution fusion | flops 1259223808 | bytes 11285508 | tf_op jit(solution)/shard_map/dot_general | solution.py:25
  155.2 9.0 %psum.7 = f32[1280]{0:T(1024)S(1)} all-reduce(f32[1280]{0:T(1024)S(1)} %get-tuple-element.57), channel_id=1, replica_groups=mesh['rep'=8,'seq'=4] {'seq'}, use_global_device_ids=true, to_apply=%region_1.0 | all-reduce | flops 1280 | bytes 10240 | tf_op jit(solution)/shard_map/psum | solution.py:521
  164.2 0.6 multiply_reduce_fusion
  166.9 6.7 %multiply_convert_fusion = (bf16[192,2432]{1,0:T(8,128)(2,1)S(1)}, f32[192,2432]{1,0:T(8,128)}) fusion(f32[]{:T(128)S(6)} %neg.3, bf16[2432,1280]{1,0:T(8,128)(2,1)} %param.25, f32[192,1280]{1,0:T(8,128)} %get-tuple-element.58, f32[1280]{0:T(1024)S(1)} %get-tuple-element.46, f32[1280]{0:T(1024)S(1)} %get-tuple-element.45), kind=kOutput, calls=%fused_computation.21 | convolution fusion | flops 1200979968 | bytes 10020868 | tf_op jit(solution)/shard_map/dot_general | solution.py:43
  173.7 0.4 convolution_convert_fusion.6
  174.1 5.7 %fusion.45 = f32[192,1536]{1,0:T(8,128)S(1)} fusion(bf16[192,2432]{1,0:T(8,128)(2,1)S(1)} %get-tuple-element.59, bf16[1536,2432]{1,0:T(8,128)(2,1)} %all-gather.2.cloned.1.call-done), kind=kOutput, calls=%fused_computation.86 | convolution fusion | flops 1434451968 | bytes 9584640 | tf_op jit(solution)/shard_map/dot_general | solution.py:51
  179.8 0.3 fusion.9
  180.1 0.9 copy.69
  181.0 3.7 %all-to-all-start.1 = ((bf16[192,4,384]{2,0,1:T(8,128)(2,1)}), bf16[192,4,384]{2,0,1:T(8,128)(2,1)S(1)}, u32[]{:S(2)}, u32[]{:S(2)}) async-start(bf16[192,4,384]{2,0,1:T(8,128)(2,1)} %bitcast.72), calls=%async_computation.1 | async-start | bytes 1179648 | tf_op jit(solution)/shard_map/all_to_all | solution.py:526
  184.7 0.3 convolution_convert_fusion
  185.0 0.5 reshape.86
  185.5 0.2 convolution_convert_fusion.2
  185.7 0.2 reshape.85
  186.0 5.5 %all-to-all-done.1 = bf16[192,4,384]{2,0,1:T(8,128)(2,1)S(1)} async-done(((bf16[192,4,384]{2,0,1:T(8,128)(2,1)}), bf16[192,4,384]{2,0,1:T(8,128)(2,1)S(1)}, u32[]{:S(2)}, u32[]{:S(2)}) %all-to-all-start.1) | async-done | bytes 589856 | tf_op jit(solution)/shard_map/all_to_all | solution.py:526
  191.5 0.8 copy-done.5
  192.3 22.3 %attend_back.1 = bf16[768,1152]{1,0:T(8,128)(2,1)} custom-call(f32[768,1152]{1,0:T(8,128)} %convolution_add_fusion.1.joined_ref, bf16[768,384]{1,0:T(8,128)(2,1)} %get-tuple-element.22.q_ref, bf16[896,384]{1,0:T(8,128)(2,1)} %get-tuple-element.23.k_ref, bf16[896,384]{1,0:T(8,128)(2,1)} %get-tuple-element.24.v_ref, f32[3,6,256]{2,1,0:T(8,128)} %get-tuple-element.25.inv_ref, ...), custom_call_target="tpu_custom_call" | custom-call | tf_op jit(solution)/shard_map/attend_back/pallas_call | solution.py:200
  214.6 2.0 convolution_convert_fusion.3
  216.6 2.1 convolution_convert_fusion.4
  218.8 9.9 %fusion.46 = f32[768,2432]{1,0:T(8,128)} fusion(bf16[768,1152]{1,0:T(8,128)(2,1)S(1)} %copy-done.4, bf16[2432,1152]{1,0:T(8,128)(2,1)} %bitcast.90), kind=kOutput, calls=%fused_computation.87 | convolution fusion | flops 4303355904 | bytes 14843904 | tf_op jit(solution)/shard_map/dot_general | solution.py:532
  228.7 0.1 reshape.89
  228.7 0.2 broadcast_in_dim.19
  228.9 2.9 dynamic_update_slice.3
  231.8 0.7 reshape.84
  232.5 1.8 concatenate.22
  234.4 0.1 slice.42
  234.4 2.8 convolution_convert_fusion.1
  237.2 1.2 reshape.82
  238.5 1.3 fusion.10
  239.8 2.2 copy.47
  242.0 2.7 copy.68
  244.7 6.4 %fusion.41 = (f32[768]{0:T(1024)S(1)}, f32[768]{0:T(1024)S(1)}, f32[768,2432]{1,0:T(8,128)S(1)}) fusion(bf16[4,192,2432]{2,1,0:T(8,128)(2,1)} %get-tuple-element.18, f32[768,2432]{1,0:T(8,128)} %fusion.46, bf16[768,64]{0,1:T(8,128)(2,1)S(1)} %convolution_convert_fusion.4, bf16[2432,64]{0,1:T(8,128)(2,1)S(1)} %copy-done.9), kind=kOutput, calls=%fused_computation.82 | convolution fusion | flops 248412672 | bytes 19093504 | tf_op jit(solution)/shard_map/dot_general | solution.py:534
  251.1 1.8 fusion.2
  252.9 2.9 fusion.8.lat_ref
  255.8 93.4 %reduce_all.1 = (f32[24,2432]{1,0:T(8,128)}, f32[4,172,128]{2,1,0:T(8,128)}) custom-call(bf16[2,4,4,24,2432]{4,3,2,1,0:T(8,128)(2,1)} %fusion.8.lat_ref, bf16[2,4,4,172,128]{4,3,2,1,0:T(8,128)(2,1)} %bitcast.77), custom_call_target="tpu_custom_call" | custom-call | tf_op jit(solution)/shard_map/reduce_all/pallas_call | solution.py:338
  349.2 1.1 reshape.88
  350.3 0.2 fusion.42
  350.4 0.1 slice_bitcast_fusion
  350.5 0.1 slice.46
  350.7 0.8 copy.50
  351.5 0.8 copy.49
  352.2 0.8 copy.52
  353.0 0.7 copy.51
  353.7 0.7 copy.73
  (31 shorter events, 0.1 us)
Async XLA Ops:
  7.2 1.2 copy-start
  7.2 135.7 %all-gather.2.cloned.1.call-start = ((), (), s32[]{:S(2)}) async-start(), calls=%async_computation.2 | async-start | bytes 7704576 | tf_op jit(solution)/shard_map/all_gather | solution.py:500
  13.3 84.9 %copy-start.8 = (bf16[2432,64]{0,1:T(8,128)(2,1)S(1)}, bf16[2432,64]{0,1:T(8,128)(2,1)}, u32[]{:S(2)}) copy-start(bf16[2432,64]{0,1:T(8,128)(2,1)} %param.20) | copy-start | bytes 933892
  98.2 4.0 %copy-start.2 = (bf16[4,192,2432]{2,1,0:T(8,128)(2,1)S(1)}, bf16[4,192,2432]{2,1,0:T(8,128)(2,1)}, u32[]{:S(2)}) copy-start(bf16[4,192,2432]{2,1,0:T(8,128)(2,1)} %get-tuple-element.18) | copy-start | bytes 11206660
  112.4 20.6 %copy-start.12 = (f32[4,192,128]{2,1,0:T(8,128)S(1)}, f32[4,192,128]{2,1,0:T(8,128)}, u32[]{:S(2)}) copy-start(f32[4,192,128]{2,1,0:T(8,128)} %get-tuple-element.21) | copy-start | bytes 1179652
  112.4 30.1 %copy-start.11 = (bf16[1536,64]{0,1:T(8,128)(2,1)S(1)}, bf16[1536,64]{0,1:T(8,128)(2,1)}, u32[]{:S(2)}) copy-start(bf16[1536,64]{0,1:T(8,128)(2,1)} %param.23) | copy-start | bytes 589828
  129.3 13.1 %all-to-all-start = ((bf16[4,192,384]{2,1,0:T(8,128)(2,1)}), bf16[4,192,384]{2,1,0:T(8,128)(2,1)S(1)}, u32[]{:S(2)}, u32[]{:S(2)}) async-start(bf16[4,192,384]{2,1,0:T(8,128)(2,1)} %bitcast.86), calls=%async_computation | async-start | bytes 1179648 | tf_op jit(solution)/shard_map/all_to_all | solution.py:517
  142.8 6.3 %copy-start.6 = (f32[192,2432]{1,0:T(8,128)S(1)}, f32[192,2432]{1,0:T(8,128)}, u32[]{:S(2)}) copy-start(f32[192,2432]{1,0:T(8,128)} %get-tuple-element.17) | copy-start | bytes 5603332
  142.8 6.3 %copy-start.10 = (bf16[64,2432]{1,0:T(8,128)(2,1)S(1)}, bf16[64,2432]{1,0:T(8,128)(2,1)}, u32[]{:S(2)}) copy-start(bf16[64,2432]{1,0:T(8,128)(2,1)} %param.24) | copy-start | bytes 933892
  149.1 15.1 %copy-start.14 = (f32[1280]{0:T(1024)S(1)}, f32[1280]{0:T(1024)}, u32[]{:S(2)}) copy-start(f32[1280]{0:T(1024)} %param.18) | copy-start | bytes 15364
  181.0 10.5 %all-to-all-start.1 = ((bf16[192,4,384]{2,0,1:T(8,128)(2,1)}), bf16[192,4,384]{2,0,1:T(8,128)(2,1)S(1)}, u32[]{:S(2)}, u32[]{:S(2)}) async-start(bf16[192,4,384]{2,0,1:T(8,128)(2,1)} %bitcast.72), calls=%async_computation.1 | async-start | bytes 1179648 | tf_op jit(solution)/shard_map/all_to_all | solution.py:526
  191.5 0.8 copy-start.5
  214.6 4.2 %copy-start.4 = (bf16[768,1152]{1,0:T(8,128)(2,1)S(1)}, bf16[768,1152]{1,0:T(8,128)(2,1)}, u32[]{:S(2)}) copy-start(bf16[768,1152]{1,0:T(8,128)(2,1)} %attend_back.1) | copy-start | bytes 5308420
  239.8 4.9 %copy-start.9 = (bf16[2432,64]{0,1:T(8,128)(2,1)S(1)}, bf16[2432,64]{0,1:T(8,128)(2,1)}, u32[]{:S(2)}) copy-start(bf16[2432,64]{0,1:T(8,128)(2,1)} %param.20) | copy-start | bytes 933892
  244.7 6.4 %copy-start.3 = (bf16[4,192,2432]{2,1,0:T(8,128)(2,1)S(1)}, bf16[4,192,2432]{2,1,0:T(8,128)(2,1)}, u32[]{:S(2)}) copy-start(bf16[4,192,2432]{2,1,0:T(8,128)(2,1)} %get-tuple-element.18) | copy-start | bytes 11206660
  251.1 1.8 copy-start.7
  255.8 98.6 %copy-start.1 = (bf16[192,2432]{1,0:T(8,128)(2,1)S(1)}, bf16[192,2432]{1,0:T(8,128)(2,1)}, u32[]{:S(2)}) copy-start(bf16[192,2432]{1,0:T(8,128)(2,1)} %param.22) | copy-start | bytes 2801668
  349.2 4.5 %copy-start.13 = (f32[24,2432]{1,0:T(8,128)S(1)}, f32[24,2432]{1,0:T(8,128)}, u32[]{:S(2)}) copy-start(f32[24,2432]{1,0:T(8,128)} %get-tuple-element.71) | copy-start | bytes 700420
Sparse Core Ops, SparseCore 0:
  11.5 126.2 all-gather.1
